TPU v7x, 128 devices: a whole 4x4x4 slice. The times are simulated.
128 devices in a mesh: gy: 4 (over y_hi, core), gz: 8 (over y_lo, x), fsdp: 4 (over z).
Axes of the slice: x: 4, y: 4 (y_hi: 2, y_lo: 2; y = y_hi * 2 + y_lo), z: 4, core: 2. Of those that a mesh axis runs over, the one named last changes fastest.
Arguments:
- coarse_field: bfloat16 [4, 48, 16, 64, 128], P('fsdp', None, 'gy', 'gz'), may hold values from -6 to 6
- fine_target: bfloat16 [4, 48, 16, 64, 128], P('fsdp', None, 'gy', 'gz'), may hold values from -6 to 6
- kernel_one: float32 [48, 1296], P(None, 'fsdp'), may hold values from -0.15625 to 0.15625
- kernel_two: float32 [48, 1296], P(None, 'fsdp'), may hold values from -0.15625 to 0.15625
- moment_one: float32 [48, 1296], P(None, 'fsdp'), may hold values from -0.0018 to 0.0018
- moment_two: float32 [48, 1296], P(None, 'fsdp'), may hold values from -0.0018 to 0.0018
- second_one: float32 [48, 1296], P(None, 'fsdp'), may hold values from 1e-09 to 1e-07
- second_two: float32 [48, 1296], P(None, 'fsdp'), may hold values from 1e-09 to 1e-07
Outputs:
- prediction: bfloat16 [4, 48, 16, 64, 128], P('fsdp', None, 'gy', 'gz')
- update_one: float32 [48, 1296], P(None, 'fsdp')
- update_two: float32 [48, 1296], P(None, 'fsdp')
All inputs are finite; a program needn't handle non-finite values.
Results may differ from a plain program's by a relative error of at most 0.0049.
Values may be sent and summed in bfloat16 or wider, within the bound.
A program may use at most 128 MiB of HBM per device.

v0:
```python
import jax
import jax.numpy as jnp
from jax import lax
from jax.experimental import pallas as pl
from jax.experimental.pallas import tpu as pltpu
from jax.sharding import PartitionSpec as P

first_bias = 0.9999734386011124
second_bias = 0.09520785288629038

C = 48
TY, TZ, XL = 4, 8, 128
GY, GZ, NF = 4, 8, 4
PLANE = GY * GZ
TAPS = 27 * C
COLS = TAPS // NF
K9 = 9 * C
C3 = 3 * C
MESH = pl.DeviceIdType.MESH
f32, bf16 = jnp.float32, jnp.bfloat16
DIRS = [(0, -1), (0, 1), (-1, 0), (1, 0), (-1, -1), (-1, 1), (1, -1), (1, 1)]


def edge(step, size, sending):
    if step == 0:
        return pl.ds(1, size)
    if sending:
        return pl.ds(1 if step < 0 else size, 1)
    return pl.ds(size + 1 if step < 0 else 0, 1)


def inside(value, count):
    return jnp.logical_and(value >= 0, value < count)


def roll_right(v, lane):
    return jnp.where(lane > 0, pltpu.roll(v, 1, 1), 0.0)


def roll_left(v, lane):
    return jnp.where(lane < XL - 1, pltpu.roll(v, XL - 1, 1), 0.0)


def rows9(buf, y, za, zb):
    parts = []
    for dy in range(3):
        a = buf[y + dy, pl.ds(za, 3)].reshape(C3, XL)
        b = buf[y + dy, pl.ds(zb, 3)].reshape(C3, XL)
        parts.append(jnp.concatenate([a, b], 1))
    return jnp.concatenate(parts, 0)


def interior(n):
    z = 1 + 2 * (n % 3)
    return 1 + n // 3, z, z + 1


def rim(n):
    plane = n < 8
    y = jnp.where(plane, 3 * (n // 4), n - 7)
    za = jnp.where(plane, 2 * (n % 4), 0)
    zb = jnp.where(plane, za + 1, TZ - 1)
    return y, za, zb


def every(n):
    z = 2 * (n % 4)
    return n // 4, z, z + 1


def kernel(
    x_ref, t_ref, k1_ref, k2_ref, m1_ref, m2_ref, s1_ref, s2_ref,
    pred_ref, u1_ref, u2_ref,
    X, H, E, E1, A1, TG, TS, PS, WG, W1, W2, WB, D, P1, P2, R, Z, TT, Q, A,
    hs, hr, ws, wr, gs, gr, zs, zr, qs, qr,
):
    gy = lax.axis_index("gy")
    gz = lax.axis_index("gz")
    fs = lax.axis_index("fsdp")
    core = gy % 2
    place = gy * GZ + gz
    tile = (gy // 2) * GZ + gz
    lane = lax.broadcasted_iota(jnp.int32, (C, XL), 1)

    def plane_device(index):
        return (index // GZ, index % GZ, fs)

    barrier = pltpu.get_barrier_semaphore()

    def greet(n, carry):
        pl.semaphore_signal(
            barrier, inc=1, device_id=plane_device((place + n) % PLANE), device_id_type=MESH
        )
        return carry

    lax.fori_loop(1, PLANE, greet, 0)
    for n in range(1, NF):
        pl.semaphore_signal(
            barrier, inc=1, device_id=(gy, gz, (fs + n) % NF), device_id_type=MESH
        )

    for k, ref in enumerate((k1_ref, k2_ref)):
        WG[k, fs] = jnp.zeros((C, 384), bf16)
        WG[k, fs, :, 0:COLS] = ref[...].astype(bf16)
    for y in range(TY):
        TS[y] = x_ref[:, y].astype(f32).reshape(C * TZ, XL)
        for z in range(TZ):
            X[y + 1, z + 1] = TS[y, pl.ds(z, C, stride=TZ), :].astype(bf16)

    send_ok = [
        jnp.logical_and(inside(gy + dy, GY), inside(gz + dz, GZ)) for dy, dz in DIRS
    ]
    recv_ok = [
        jnp.logical_and(inside(gy - dy, GY), inside(gz - dz, GZ)) for dy, dz in DIRS
    ]

    for d, (dy, dz) in enumerate(DIRS):
        at = (edge(dy, TY, False), edge(dz, TZ, False))

        @pl.when(jnp.logical_not(recv_ok[d]))
        def _():
            for buf in (X, H, E):
                region = buf.at[at]
                region[...] = jnp.zeros(region.shape, bf16)

    def halo(buf, phase, d):
        dy, dz = DIRS[d]
        return pltpu.make_async_remote_copy(
            src_ref=buf.at[edge(dy, TY, True), edge(dz, TZ, True)],
            dst_ref=buf.at[edge(dy, TY, False), edge(dz, TZ, False)],
            send_sem=hs.at[phase, d],
            recv_sem=hr.at[phase, d],
            device_id=(
                jnp.clip(gy + dy, 0, GY - 1), jnp.clip(gz + dz, 0, GZ - 1), fs
            ),
            device_id_type=MESH,
        )

    def halo_start(buf, phase):
        for d in range(8):
            @pl.when(send_ok[d])
            def _():
                halo(buf, phase, d).start()

    def halo_recv(buf, phase):
        for d in range(8):
            @pl.when(recv_ok[d])
            def _():
                halo(buf, phase, d).wait_recv()

    def halo_sent(buf, phase):
        for d in range(8):
            @pl.when(send_ok[d])
            def _():
                halo(buf, phase, d).wait_send()

    def weight(k, n, owner):
        return pltpu.make_async_remote_copy(
            src_ref=WG.at[k, owner],
            dst_ref=WG.at[k, owner],
            send_sem=ws.at[k, n - 1],
            recv_sem=wr.at[k, n - 1],
            device_id=(gy, gz, (fs + n) % NF),
            device_id_type=MESH,
        )

    pl.semaphore_wait(barrier, PLANE - 1 + NF - 1)

    for n in range(1, NF):
        weight(0, n, fs).start()
    halo_start(X, 0)
    for n in range(1, NF):
        weight(1, n, fs).start()

    for y in range(TY):
        TS[y] = t_ref[:, y].astype(f32).reshape(C * TZ, XL)
        for z in range(TZ):
            TG[y, z] = TS[y, pl.ds(z, C, stride=TZ), :]

    def gathered(k):
        return jnp.concatenate([WG[k, f].astype(f32)[:, :COLS] for f in range(NF)], 1)

    def forward_matrix(full, out):
        for dx in range(3):
            out[dx * C:dx * C + C, :] = jnp.concatenate(
                [full[:, (3 * g + dx) * C:(3 * g + dx + 1) * C] for g in range(9)], 1
            ).astype(bf16)

    for n in range(1, NF):
        weight(0, n, (fs - n + NF) % NF).wait_recv()
    forward_matrix(gathered(0), W1)

    def conv(w, buf, y, za, zb, back):
        out = jnp.dot(w[...], rows9(buf, y, za, zb), preferred_element_type=f32)
        res = []
        for h in range(2):
            q = out[:, h * XL:(h + 1) * XL]
            low, mid, high = q[:C], q[C:2 * C], q[2 * C:]
            if back:
                low, high = high, low
            res.append(mid + roll_right(low, lane) + roll_left(high, lane))
        return res

    def conv1(where):
        def body(n, carry):
            y, za, zb = where(n)
            for z, a1 in zip((za, zb), conv(W1, X, y, za, zb, False)):
                A1[y, z] = a1
                H[y + 1, z + 1] = jnp.maximum(a1, 0.0).astype(bf16)
            return carry
        return body

    halo_recv(X, 0)
    lax.fori_loop(0, 10, conv1(rim), 0, unroll=2)
    halo_start(H, 1)
    lax.fori_loop(0, 6, conv1(interior), 0, unroll=2)

    for n in range(1, NF):
        weight(1, n, (fs - n + NF) % NF).wait_recv()
    full2 = gathered(1)
    forward_matrix(full2, W2)

    def conv2(where):
        def body(n, carry):
            y, za, zb = where(n)
            for z, a2 in zip((za, zb), conv(W2, H, y, za, zb, False)):
                total = X[y + 1, z + 1].astype(f32) + a2
                PS[y, pl.ds(z, C, stride=TZ), :] = total
                E[y + 1, z + 1] = (total - TG[y, z]).astype(bf16)
            return carry
        return body

    lax.fori_loop(0, 6, conv2(interior), 0, unroll=2)
    halo_recv(H, 1)
    lax.fori_loop(0, 10, conv2(rim), 0, unroll=2)
    halo_start(E, 2)

    def shifted(e):
        v = e.astype(f32)
        return jnp.concatenate(
            [roll_left(v, lane).astype(bf16), e, roll_right(v, lane).astype(bf16)], 0
        )

    def weight_grad(buf, err):
        D[...] = jnp.zeros((C3, K9), f32)

        def body(n, carry):
            y, za, zb = every(n)
            left = jnp.concatenate([shifted(err(y, za)), shifted(err(y, zb))], 1)
            D[...] += lax.dot_general(
                left, rows9(buf, y, za, zb), (((1,), (1,)), ((), ())),
                preferred_element_type=f32,
            )
            return carry

        lax.fori_loop(0, 16, body, 0, unroll=2)

    def pack(out):
        grad = D[...]
        for f in range(NF):
            pieces = []
            for third in range(3):
                col = COLS * f
                while col < COLS * (f + 1):
                    block, i = col // C, col % C
                    width = min(C - i, COLS * (f + 1) - col)
                    g, dx = block // 3, block % 3
                    pieces.append(
                        grad[dx * C + 16 * third:dx * C + 16 * third + 16,
                             g * C + i:g * C + i + width]
                    )
                    col += width
            pieces.append(jnp.zeros((16, 1024 - 3 * COLS), f32))
            flat = jnp.concatenate(pieces, 1)
            for t in range(16):
                out[t, f] = flat[(t // 8) * 8:(t // 8) * 8 + 8, (t % 8) * 128:(t % 8 + 1) * 128]

    def scatter(k, src):
        def send(n, carry):
            to = (tile + n) % 16
            owner = (2 * (to // GZ) + k) * GZ + to % GZ
            pltpu.make_async_remote_copy(
                src_ref=src.at[to],
                dst_ref=R.at[(place - owner + PLANE) % PLANE],
                send_sem=gs.at[k],
                recv_sem=gr,
                device_id=plane_device(owner),
                device_id_type=MESH,
            ).start()
            return carry

        @pl.when(core == k)
        def _():
            R[0] = src[tile]

        @pl.when(core != k)
        def _():
            send(0, 0)

        lax.fori_loop(1, 16, send, 0)

    def scattered(k, src):
        def wait(count):
            pltpu.make_async_remote_copy(
                src_ref=src.at[pl.ds(0, count)], dst_ref=R.at[pl.ds(0, count)],
                send_sem=gs.at[k], recv_sem=gr, device_id=plane_device(place),
                device_id_type=MESH,
            ).wait_send()

        @pl.when(core == k)
        def _():
            wait(15)

        @pl.when(core != k)
        def _():
            wait(16)

    weight_grad(H, lambda y, z: E[y + 1, z + 1])
    pack(P2)
    scatter(1, P2)

    turned = full2.T
    for dx in range(3):
        WB[dx * C:dx * C + C, :] = jnp.concatenate(
            [
                turned[(26 - 3 * g - 2 + dx) * C:(26 - 3 * g - 2 + dx + 1) * C, :]
                for g in range(9)
            ],
            1,
        ).astype(bf16)

    halo_recv(E, 2)

    def back(n, carry):
        y, za, zb = every(n)
        for z, b in zip((za, zb), conv(WB, E, y, za, zb, True)):
            E1[y, z] = jnp.where(A1[y, z] > 0, b, 0.0).astype(bf16)
        return carry

    lax.fori_loop(0, 16, back, 0, unroll=2)
    weight_grad(X, lambda y, z: E1[y, z])
    pack(P1)
    scatter(0, P1)

    for y in range(TY):
        pred_ref[:, y] = PS[y].reshape(C, TZ, XL).astype(bf16)

    pltpu.make_async_remote_copy(
        src_ref=R.at[pl.ds(1, PLANE - 1)], dst_ref=R.at[pl.ds(1, PLANE - 1)],
        send_sem=gs.at[0], recv_sem=gr, device_id=plane_device(place), device_id_type=MESH,
    ).wait_recv()
    own = R[0]
    for n in range(1, PLANE):
        own = own + R[n]
    Z[fs] = own
    for n in range(1, NF):
        pltpu.make_async_remote_copy(
            src_ref=Z.at[fs], dst_ref=Z.at[fs], send_sem=zs.at[n - 1], recv_sem=zr.at[n - 1],
            device_id=(gy, gz, (fs + n) % NF), device_id_type=MESH,
        ).start()
    for n in range(1, NF):
        other = (fs - n + NF) % NF
        pltpu.make_async_remote_copy(
            src_ref=Z.at[other], dst_ref=Z.at[other], send_sem=zs.at[n - 1],
            recv_sem=zr.at[n - 1], device_id=(gy, gz, other), device_id_type=MESH,
        ).wait_recv()
    total = Z[0] + Z[1] + Z[2] + Z[3]
    TT[...] = total
    Q[0] = TT[fs]
    Q[1] = jnp.sum(total * total, 0)

    slot = core * 16 + tile
    A[slot] = Q[...]

    def spread(n, carry):
        pltpu.make_async_remote_copy(
            src_ref=Q, dst_ref=A.at[slot], send_sem=qs, recv_sem=qr,
            device_id=plane_device((place + n) % PLANE), device_id_type=MESH,
        ).start()
        return carry

    lax.fori_loop(1, PLANE, spread, 0)
    gather = pltpu.make_async_remote_copy(
        src_ref=A.at[pl.ds(0, PLANE - 1)], dst_ref=A.at[pl.ds(0, PLANE - 1)],
        send_sem=qs, recv_sem=qr, device_id=plane_device(place), device_id_type=MESH,
    )
    gather.wait_recv()

    squares = A[0, 1]
    for n in range(1, PLANE):
        squares = squares + A[n, 1]
    norm = jnp.sqrt(jnp.sum(squares, keepdims=True))
    factor = jnp.minimum(1.0, 1.0 / (norm + 1e-06))
    for k, (m_ref, s_ref, u_ref) in enumerate(
        ((m1_ref, s1_ref, u1_ref), (m2_ref, s2_ref, u2_ref))
    ):
        flat = jnp.concatenate(
            [
                jnp.concatenate([A[k * 16 + r * 8 + t, 0] for t in range(8)], 1)
                for r in range(2)
            ],
            0,
        )
        for third in range(3):
            at = pl.ds(16 * third, 16)
            grad = factor * flat[:, COLS * third:COLS * (third + 1)]
            first = 0.9 * m_ref[at, :] + 0.1 * grad
            second = 0.999 * s_ref[at, :] + 0.001 * grad * grad
            u_ref[at, :] = first / first_bias / (jnp.sqrt(second / second_bias) + 1e-08)

    for n in range(1, NF):
        weight(0, n, fs).wait_send()
        weight(1, n, fs).wait_send()
        pltpu.make_async_remote_copy(
            src_ref=Z.at[fs], dst_ref=Z.at[fs], send_sem=zs.at[n - 1], recv_sem=zr.at[n - 1],
            device_id=(gy, gz, (fs + n) % NF), device_id_type=MESH,
        ).wait_send()
    for phase, buf in enumerate((X, H, E)):
        halo_sent(buf, phase)
    scattered(0, P1)
    scattered(1, P2)
    gather.wait_send()


def shards(
    coarse_field, fine_target, kernel_one, kernel_two,
    moment_one, moment_two, second_one, second_two,
):
    vmem = pl.BlockSpec(memory_space=pltpu.VMEM)
    dma = pltpu.SemaphoreType.DMA
    padded = pltpu.VMEM((TY + 2, TZ + 2, C, XL), bf16)
    prediction, update_one, update_two = pl.pallas_call(
        kernel,
        out_shape=[
            jax.ShapeDtypeStruct((C, TY, TZ, XL), bf16),
            jax.ShapeDtypeStruct((C, COLS), f32),
            jax.ShapeDtypeStruct((C, COLS), f32),
        ],
        in_specs=[vmem] * 8,
        out_specs=[vmem] * 3,
        scratch_shapes=[
            padded, padded, padded,
            pltpu.VMEM((TY, TZ, C, XL), bf16),
            pltpu.VMEM((TY, TZ, C, XL), f32),
            pltpu.VMEM((TY, TZ, C, XL), f32),
            pltpu.VMEM((TY, C * TZ, XL), f32),
            pltpu.VMEM((TY, C * TZ, XL), f32),
            pltpu.VMEM((2, NF, C, 384), bf16),
            pltpu.VMEM((C3, K9), bf16),
            pltpu.VMEM((C3, K9), bf16),
            pltpu.VMEM((C3, K9), bf16),
            pltpu.VMEM((C3, K9), f32),
            pltpu.VMEM((16, NF, 8, 128), f32),
            pltpu.VMEM((16, NF, 8, 128), f32),
            pltpu.VMEM((PLANE, NF, 8, 128), f32),
            pltpu.VMEM((NF, NF, 8, 128), f32),
            pltpu.VMEM((NF, 8, 128), f32),
            pltpu.VMEM((2, 8, 128), f32),
            pltpu.VMEM((PLANE, 2, 8, 128), f32),
            dma((3, 8)), dma((3, 8)),
            dma((2, 3)), dma((2, 3)),
            dma((2,)), dma,
            dma((3,)), dma((3,)),
            dma, dma,
        ],
        compiler_params=pltpu.CompilerParams(
            collective_id=0, has_side_effects=True, vmem_limit_bytes=40 << 20
        ),
    )(
        coarse_field[0], fine_target[0], kernel_one, kernel_two,
        moment_one, moment_two, second_one, second_two,
    )
    return prediction[None], update_one, update_two


def solution(mesh):
    field = P("fsdp", None, "gy", "gz", None)
    state = P(None, "fsdp")
    return jax.shard_map(
        shards,
        mesh=mesh,
        in_specs=(field, field) + (state,) * 6,
        out_specs=(field, state, state),
        check_vma=False,
    )
```

profile of v0, /device:TPU:1, one launch (start us, length us, event | category | flops | bytes accessed | tf_op | source)
XLA Modules:
  0.0 60.7 jit_solution(897279669142678545)
XLA Ops:
  0.6 0.0 copy-start
  0.6 1.0 %copy-done = bf16[1,48,4,8,128]{4,3,2,1,0:T(8,128)(2,1)S(1)} copy-done((bf16[1,48,4,8,128]{4,3,2,1,0:T(8,128)(2,1)S(1)}, bf16[1,48,4,8,128]{4,3,2,1,0:T(8,128)(2,1)}, u32[]{:S(2)}) %copy-start) | copy-done | bytes 393240
  1.6 0.0 copy-start.1
  1.6 1.0 %copy-done.1 = bf16[1,48,4,8,128]{4,3,2,1,0:T(8,128)(2,1)S(1)} copy-done((bf16[1,48,4,8,128]{4,3,2,1,0:T(8,128)(2,1)S(1)}, bf16[1,48,4,8,128]{4,3,2,1,0:T(8,128)(2,1)}, u32[]{:S(2)}) %copy-start.1) | copy-done | bytes 393240
  2.6 0.0 copy-start.2
  2.6 0.9 %copy-done.2 = f32[48,324]{1,0:T(8,128)S(1)} copy-done((f32[48,324]{1,0:T(8,128)S(1)}, f32[48,324]{1,0:T(8,128)}, u32[]{:S(2)}) %copy-start.2) | copy-done | bytes 62232
  3.5 0.0 copy-start.3
  3.5 0.9 %copy-done.3 = f32[48,324]{1,0:T(8,128)S(1)} copy-done((f32[48,324]{1,0:T(8,128)S(1)}, f32[48,324]{1,0:T(8,128)}, u32[]{:S(2)}) %copy-start.3) | copy-done | bytes 62232
  4.4 0.0 copy-start.4
  4.4 0.9 %copy-done.4 = f32[48,324]{1,0:T(8,128)S(1)} copy-done((f32[48,324]{1,0:T(8,128)S(1)}, f32[48,324]{1,0:T(8,128)}, u32[]{:S(2)}) %copy-start.4) | copy-done | bytes 62232
  5.3 0.0 copy-start.5
  5.3 0.9 %copy-done.5 = f32[48,324]{1,0:T(8,128)S(1)} copy-done((f32[48,324]{1,0:T(8,128)S(1)}, f32[48,324]{1,0:T(8,128)}, u32[]{:S(2)}) %copy-start.5) | copy-done | bytes 62232
  6.2 0.0 copy-start.6
  6.2 0.9 %copy-done.6 = f32[48,324]{1,0:T(8,128)S(1)} copy-done((f32[48,324]{1,0:T(8,128)S(1)}, f32[48,324]{1,0:T(8,128)}, u32[]{:S(2)}) %copy-start.6) | copy-done | bytes 62232
  7.0 0.0 copy-start.7
  7.1 0.9 %copy-done.7 = f32[48,324]{1,0:T(8,128)S(1)} copy-done((f32[48,324]{1,0:T(8,128)S(1)}, f32[48,324]{1,0:T(8,128)}, u32[]{:S(2)}) %copy-start.7) | copy-done | bytes 62232
  7.9 50.8 %shard_map.103 = (bf16[48,4,8,128]{3,2,1,0:T(8,128)(2,1)S(1)}, f32[48,324]{1,0:T(8,128)S(1)}, f32[48,324]{1,0:T(8,128)S(1)}) custom-call(bf16[48,4,8,128]{3,2,1,0:T(8,128)(2,1)S(1)} %bitcast.4, bf16[48,4,8,128]{3,2,1,0:T(8,128)(2,1)S(1)} %bitcast.5, f32[48,324]{1,0:T(8,128)S(1)} %copy-done.2, f32[48,324]{1,0:T(8,128)S(1)} %copy-done.3, ...), custom_call_target="tpu_custom_call" | custom-call | tf_op jit(solution)/shard_map/pallas_call | solution.py:432
  58.7 0.7 %copy.14 = bf16[1,48,4,8,128]{4,3,2,1,0:T(8,128)(2,1)} copy(bf16[1,48,4,8,128]{4,3,2,1,0:T(8,128)(2,1)S(1)} %bitcast.3) | data formatting | bytes 786432
  59.5 0.6 %copy.15 = f32[48,324]{1,0:T(8,128)} copy(f32[48,324]{1,0:T(8,128)S(1)} %get-tuple-element.13) | data formatting | bytes 124416
  60.1 0.6 %copy.16 = f32[48,324]{1,0:T(8,128)} copy(f32[48,324]{1,0:T(8,128)S(1)} %get-tuple-element.14) | data formatting | bytes 124416
Async XLA Ops:
  0.6 1.0 %copy-start = (bf16[1,48,4,8,128]{4,3,2,1,0:T(8,128)(2,1)S(1)}, bf16[1,48,4,8,128]{4,3,2,1,0:T(8,128)(2,1)}, u32[]{:S(2)}) copy-start(bf16[1,48,4,8,128]{4,3,2,1,0:T(8,128)(2,1)} %param.8) | copy-start | bytes 1179652
  1.6 1.0 %copy-start.1 = (bf16[1,48,4,8,128]{4,3,2,1,0:T(8,128)(2,1)S(1)}, bf16[1,48,4,8,128]{4,3,2,1,0:T(8,128)(2,1)}, u32[]{:S(2)}) copy-start(bf16[1,48,4,8,128]{4,3,2,1,0:T(8,128)(2,1)} %param.9) | copy-start | bytes 1179652
  2.6 0.9 %copy-start.2 = (f32[48,324]{1,0:T(8,128)S(1)}, f32[48,324]{1,0:T(8,128)}, u32[]{:S(2)}) copy-start(f32[48,324]{1,0:T(8,128)} %k1_ref.1) | copy-start | bytes 186628
  3.5 0.9 %copy-start.3 = (f32[48,324]{1,0:T(8,128)S(1)}, f32[48,324]{1,0:T(8,128)}, u32[]{:S(2)}) copy-start(f32[48,324]{1,0:T(8,128)} %k2_ref.1) | copy-start | bytes 186628
  4.4 0.9 %copy-start.4 = (f32[48,324]{1,0:T(8,128)S(1)}, f32[48,324]{1,0:T(8,128)}, u32[]{:S(2)}) copy-start(f32[48,324]{1,0:T(8,128)} %m1_ref.1) | copy-start | bytes 186628
  5.3 0.9 %copy-start.5 = (f32[48,324]{1,0:T(8,128)S(1)}, f32[48,324]{1,0:T(8,128)}, u32[]{:S(2)}) copy-start(f32[48,324]{1,0:T(8,128)} %m2_ref.1) | copy-start | bytes 186628
  6.2 0.9 %copy-start.6 = (f32[48,324]{1,0:T(8,128)S(1)}, f32[48,324]{1,0:T(8,128)}, u32[]{:S(2)}) copy-start(f32[48,324]{1,0:T(8,128)} %s1_ref.1) | copy-start | bytes 186628
  7.0 0.9 %copy-start.7 = (f32[48,324]{1,0:T(8,128)S(1)}, f32[48,324]{1,0:T(8,128)}, u32[]{:S(2)}) copy-start(f32[48,324]{1,0:T(8,128)} %s2_ref.1) | copy-start | bytes 186628
where the time goes:
time: 61.2 us; the launch traced here: 60.7 us
  Pallas kernels  50.8 us (83%)
  local copies, waits for them, and re-layouts  9.3 us (15%)
  between operations  0.66 us (1%)
    pallas_call x1, Pallas kernels, shards(): pl.pallas_call(kernel, out_shape=[jax.ShapeDtypeStruct((C, TY, TZ, XL), b...  50.8 us
    unnamed x19, local copies, waits for them, and re-layouts  9.3 us

commit v1 on v0

--- a/solution.py
+++ b/solution.py
@@ -41,37 +41,29 @@
     return jnp.where(lane < XL - 1, pltpu.roll(v, XL - 1, 1), 0.0)
 
 
-def rows9(buf, y, za, zb):
-    parts = []
-    for dy in range(3):
-        a = buf[y + dy, pl.ds(za, 3)].reshape(C3, XL)
-        b = buf[y + dy, pl.ds(zb, 3)].reshape(C3, XL)
-        parts.append(jnp.concatenate([a, b], 1))
-    return jnp.concatenate(parts, 0)
-
-
-def interior(n):
-    z = 1 + 2 * (n % 3)
-    return 1 + n // 3, z, z + 1
-
-
-def rim(n):
-    plane = n < 8
-    y = jnp.where(plane, 3 * (n // 4), n - 7)
-    za = jnp.where(plane, 2 * (n % 4), 0)
-    zb = jnp.where(plane, za + 1, TZ - 1)
-    return y, za, zb
-
-
-def every(n):
-    z = 2 * (n % 4)
-    return n // 4, z, z + 1
+def rows9(buf, cells):
+    return jnp.concatenate(
+        [
+            jnp.concatenate(
+                [buf[y + dy, z:z + 3].reshape(C3, XL) for y, z in cells], 1
+            )
+            for dy in range(3)
+        ],
+        0,
+    )
+
+
+INNER = [((y, z), (y, z + 1)) for y in (1, 2) for z in (1, 3, 5)]
+RIM = [((y, z), (y, z + 1)) for y in (0, 3) for z in (0, 2, 4, 6)]
+RIM += [((y, 0), (y, TZ - 1)) for y in (1, 2)]
+PLANES = [tuple((y, z) for z in range(TZ)) for y in range(TY)]
 
 
 def kernel(
+    x_hbm, t_hbm, k1_hbm, k2_hbm, m1_hbm, m2_hbm, s1_hbm, s2_hbm,
+    pred_hbm, u1_hbm, u2_hbm,
     x_ref, t_ref, k1_ref, k2_ref, m1_ref, m2_ref, s1_ref, s2_ref,
-    pred_ref, u1_ref, u2_ref,
-    X, H, E, E1, A1, TG, TS, PS, WG, W1, W2, WB, D, P1, P2, R, Z, TT, Q, A,
+    pred_ref, u1_ref, u2_ref, ls, os, X, H, E, E1, A1, TG, TS, PS, WG, W1, W2, WB, P1, P2, R, Z, TT, Q, A,
     hs, hr, ws, wr, gs, gr, zs, zr, qs, qr,
 ):
     gy = lax.axis_index("gy")
@@ -82,6 +74,32 @@
     tile = (gy // 2) * GZ + gz
     lane = lax.broadcasted_iota(jnp.int32, (C, XL), 1)
 
+    loads = [
+        pltpu.make_async_copy(source, ref, ls.at[n])
+        for n, (source, ref) in enumerate((
+            (k1_hbm, k1_ref), (x_hbm, x_ref), (k2_hbm, k2_ref), (t_hbm, t_ref),
+            (m1_hbm, m1_ref), (s1_hbm, s1_ref), (m2_hbm, m2_ref), (s2_hbm, s2_ref),
+        ))
+    ]
+    owed = {}
+
+    def settle(name):
+        owed.pop(name)()
+
+    def finish():
+        for name in list(owed):
+            settle(name)
+
+    for n, load in enumerate(loads):
+        load.start()
+        owed["load", n] = load.wait
+    stores = [
+        pltpu.make_async_copy(ref, result, os.at[n])
+        for n, (ref, result) in enumerate((
+            (pred_ref, pred_hbm), (u1_ref, u1_hbm), (u2_ref, u2_hbm)
+        ))
+    ]
+
     def plane_device(index):
         return (index // GZ, index % GZ, fs)
 
@@ -100,8 +118,10 @@
         )
 
     for k, ref in enumerate((k1_ref, k2_ref)):
+        settle(("load", 2 * k))
         WG[k, fs] = jnp.zeros((C, 384), bf16)
         WG[k, fs, :, 0:COLS] = ref[...].astype(bf16)
+    settle(("load", 1))
     for y in range(TY):
         TS[y] = x_ref[:, y].astype(f32).reshape(C * TZ, XL)
         for z in range(TZ):
@@ -137,22 +157,23 @@
         )
 
     def halo_start(buf, phase):
+        def arrived():
+            for d in range(8):
+                @pl.when(recv_ok[d])
+                def _():
+                    halo(buf, phase, d).wait_recv()
+
+        def sent():
+            for d in range(8):
+                @pl.when(send_ok[d])
+                def _():
+                    halo(buf, phase, d).wait_send()
+
         for d in range(8):
             @pl.when(send_ok[d])
             def _():
                 halo(buf, phase, d).start()
-
-    def halo_recv(buf, phase):
-        for d in range(8):
-            @pl.when(recv_ok[d])
-            def _():
-                halo(buf, phase, d).wait_recv()
-
-    def halo_sent(buf, phase):
-        for d in range(8):
-            @pl.when(send_ok[d])
-            def _():
-                halo(buf, phase, d).wait_send()
+        owed["halo", phase], owed["halo sent", phase] = arrived, sent
 
     def weight(k, n, owner):
         return pltpu.make_async_remote_copy(
@@ -164,14 +185,26 @@
             device_id_type=MESH,
         )
 
+    def weight_start(k):
+        def arrived():
+            for n in range(1, NF):
+                weight(k, n, (fs - n + NF) % NF).wait_recv()
+
+        def sent():
+            for n in range(1, NF):
+                weight(k, n, fs).wait_send()
+
+        for n in range(1, NF):
+            weight(k, n, fs).start()
+        owed["weight", k], owed["weight sent", k] = arrived, sent
+
     pl.semaphore_wait(barrier, PLANE - 1 + NF - 1)
 
-    for n in range(1, NF):
-        weight(0, n, fs).start()
+    weight_start(0)
     halo_start(X, 0)
-    for n in range(1, NF):
-        weight(1, n, fs).start()
-
+    weight_start(1)
+
+    settle(("load", 3))
     for y in range(TY):
         TS[y] = t_ref[:, y].astype(f32).reshape(C * TZ, XL)
         for z in range(TZ):
@@ -186,53 +219,45 @@
                 [full[:, (3 * g + dx) * C:(3 * g + dx + 1) * C] for g in range(9)], 1
             ).astype(bf16)
 
-    for n in range(1, NF):
-        weight(0, n, (fs - n + NF) % NF).wait_recv()
+    settle(("weight", 0))
     forward_matrix(gathered(0), W1)
 
-    def conv(w, buf, y, za, zb, back):
-        out = jnp.dot(w[...], rows9(buf, y, za, zb), preferred_element_type=f32)
+    def conv(w, buf, cells, back=False):
+        out = jnp.dot(w[...], rows9(buf, cells), preferred_element_type=f32)
         res = []
-        for h in range(2):
+        for h in range(len(cells)):
             q = out[:, h * XL:(h + 1) * XL]
             low, mid, high = q[:C], q[C:2 * C], q[2 * C:]
             if back:
                 low, high = high, low
             res.append(mid + roll_right(low, lane) + roll_left(high, lane))
-        return res
-
-    def conv1(where):
-        def body(n, carry):
-            y, za, zb = where(n)
-            for z, a1 in zip((za, zb), conv(W1, X, y, za, zb, False)):
+        return zip(cells, res)
+
+    def conv1(groups):
+        for cells in groups:
+            for (y, z), a1 in conv(W1, X, cells):
                 A1[y, z] = a1
                 H[y + 1, z + 1] = jnp.maximum(a1, 0.0).astype(bf16)
-            return carry
-        return body
-
-    halo_recv(X, 0)
-    lax.fori_loop(0, 10, conv1(rim), 0, unroll=2)
+
+    settle(("halo", 0))
+    conv1(RIM)
     halo_start(H, 1)
-    lax.fori_loop(0, 6, conv1(interior), 0, unroll=2)
-
-    for n in range(1, NF):
-        weight(1, n, (fs - n + NF) % NF).wait_recv()
+    conv1(INNER)
+
+    settle(("weight", 1))
     full2 = gathered(1)
     forward_matrix(full2, W2)
 
-    def conv2(where):
-        def body(n, carry):
-            y, za, zb = where(n)
-            for z, a2 in zip((za, zb), conv(W2, H, y, za, zb, False)):
+    def conv2(groups):
+        for cells in groups:
+            for (y, z), a2 in conv(W2, H, cells):
                 total = X[y + 1, z + 1].astype(f32) + a2
                 PS[y, pl.ds(z, C, stride=TZ), :] = total
                 E[y + 1, z + 1] = (total - TG[y, z]).astype(bf16)
-            return carry
-        return body
-
-    lax.fori_loop(0, 6, conv2(interior), 0, unroll=2)
-    halo_recv(H, 1)
-    lax.fori_loop(0, 10, conv2(rim), 0, unroll=2)
+
+    conv2(INNER)
+    settle(("halo", 1))
+    conv2(RIM)
     halo_start(E, 2)
 
     def shifted(e):
@@ -242,21 +267,16 @@
         )
 
     def weight_grad(buf, err):
-        D[...] = jnp.zeros((C3, K9), f32)
-
-        def body(n, carry):
-            y, za, zb = every(n)
-            left = jnp.concatenate([shifted(err(y, za)), shifted(err(y, zb))], 1)
-            D[...] += lax.dot_general(
-                left, rows9(buf, y, za, zb), (((1,), (1,)), ((), ())),
+        grad = jnp.zeros((K9, C3), f32)
+        for cells in PLANES:
+            right = jnp.concatenate([shifted(err(y, z)) for y, z in cells], 1)
+            grad += lax.dot_general(
+                rows9(buf, cells), right, (((1,), (1,)), ((), ())),
                 preferred_element_type=f32,
             )
-            return carry
-
-        lax.fori_loop(0, 16, body, 0, unroll=2)
-
-    def pack(out):
-        grad = D[...]
+        return grad.T
+
+    def pack(grad, out):
         for f in range(NF):
             pieces = []
             for third in range(3):
@@ -299,24 +319,29 @@
 
         lax.fori_loop(1, 16, send, 0)
 
-    def scattered(k, src):
-        def wait(count):
-            pltpu.make_async_remote_copy(
-                src_ref=src.at[pl.ds(0, count)], dst_ref=R.at[pl.ds(0, count)],
-                send_sem=gs.at[k], recv_sem=gr, device_id=plane_device(place),
-                device_id_type=MESH,
-            ).wait_send()
-
-        @pl.when(core == k)
-        def _():
-            wait(15)
-
-        @pl.when(core != k)
-        def _():
-            wait(16)
-
-    weight_grad(H, lambda y, z: E[y + 1, z + 1])
-    pack(P2)
+        def sent():
+            for count, mine in ((15, core == k), (16, core != k)):
+                @pl.when(mine)
+                def _():
+                    pltpu.make_async_remote_copy(
+                        src_ref=src.at[pl.ds(0, count)], dst_ref=R.at[pl.ds(0, count)],
+                        send_sem=gs.at[k], recv_sem=gr, device_id=plane_device(place),
+                        device_id_type=MESH,
+                    ).wait_send()
+
+        def parts():
+            @pl.when(core == k)
+            def _():
+                pltpu.make_async_remote_copy(
+                    src_ref=R.at[pl.ds(1, PLANE - 1)], dst_ref=R.at[pl.ds(1, PLANE - 1)],
+                    send_sem=gs.at[k], recv_sem=gr, device_id=plane_device(place),
+                    device_id_type=MESH,
+                ).wait_recv()
+
+        owed["parts", k], owed["scatter sent", k] = parts, sent
+
+    grad2 = weight_grad(H, lambda y, z: E[y + 1, z + 1])
+    pack(grad2, P2)
     scatter(1, P2)
 
     turned = full2.T
@@ -329,41 +354,48 @@
             1,
         ).astype(bf16)
 
-    halo_recv(E, 2)
-
-    def back(n, carry):
-        y, za, zb = every(n)
-        for z, b in zip((za, zb), conv(WB, E, y, za, zb, True)):
-            E1[y, z] = jnp.where(A1[y, z] > 0, b, 0.0).astype(bf16)
-        return carry
-
-    lax.fori_loop(0, 16, back, 0, unroll=2)
-    weight_grad(X, lambda y, z: E1[y, z])
-    pack(P1)
+    def back(groups):
+        for cells in groups:
+            for (y, z), b in conv(WB, E, cells, True):
+                E1[y, z] = jnp.where(A1[y, z] > 0, b, 0.0).astype(bf16)
+
+    back(INNER)
+    settle(("halo", 2))
+    back(RIM)
+    grad1 = weight_grad(X, lambda y, z: E1[y, z])
+    pack(grad1, P1)
     scatter(0, P1)
 
     for y in range(TY):
         pred_ref[:, y] = PS[y].reshape(C, TZ, XL).astype(bf16)
-
-    pltpu.make_async_remote_copy(
-        src_ref=R.at[pl.ds(1, PLANE - 1)], dst_ref=R.at[pl.ds(1, PLANE - 1)],
-        send_sem=gs.at[0], recv_sem=gr, device_id=plane_device(place), device_id_type=MESH,
-    ).wait_recv()
+    stores[0].start()
+    owed["store", 0] = stores[0].wait
+
+    settle(("parts", 1))
+    settle(("parts", 0))
     own = R[0]
     for n in range(1, PLANE):
         own = own + R[n]
     Z[fs] = own
+
+    def along(n, owner):
+        return pltpu.make_async_remote_copy(
+            src_ref=Z.at[owner], dst_ref=Z.at[owner], send_sem=zs.at[n - 1],
+            recv_sem=zr.at[n - 1], device_id=(gy, gz, (fs + n) % NF), device_id_type=MESH,
+        )
+
+    def sums():
+        for n in range(1, NF):
+            along(n, (fs - n + NF) % NF).wait_recv()
+
+    def sums_sent():
+        for n in range(1, NF):
+            along(n, fs).wait_send()
+
     for n in range(1, NF):
-        pltpu.make_async_remote_copy(
-            src_ref=Z.at[fs], dst_ref=Z.at[fs], send_sem=zs.at[n - 1], recv_sem=zr.at[n - 1],
-            device_id=(gy, gz, (fs + n) % NF), device_id_type=MESH,
-        ).start()
-    for n in range(1, NF):
-        other = (fs - n + NF) % NF
-        pltpu.make_async_remote_copy(
-            src_ref=Z.at[other], dst_ref=Z.at[other], send_sem=zs.at[n - 1],
-            recv_sem=zr.at[n - 1], device_id=(gy, gz, other), device_id_type=MESH,
-        ).wait_recv()
+        along(n, fs).start()
+    owed["sums"], owed["sums sent"] = sums, sums_sent
+    settle("sums")
     total = Z[0] + Z[1] + Z[2] + Z[3]
     TT[...] = total
     Q[0] = TT[fs]
@@ -384,13 +416,16 @@
         src_ref=A.at[pl.ds(0, PLANE - 1)], dst_ref=A.at[pl.ds(0, PLANE - 1)],
         send_sem=qs, recv_sem=qr, device_id=plane_device(place), device_id_type=MESH,
     )
-    gather.wait_recv()
+    owed["gather"], owed["gather sent"] = gather.wait_recv, gather.wait_send
+    settle("gather")
 
     squares = A[0, 1]
     for n in range(1, PLANE):
         squares = squares + A[n, 1]
     norm = jnp.sqrt(jnp.sum(squares, keepdims=True))
     factor = jnp.minimum(1.0, 1.0 / (norm + 1e-06))
+    for n in range(4, 8):
+        settle(("load", n))
     for k, (m_ref, s_ref, u_ref) in enumerate(
         ((m1_ref, s1_ref, u1_ref), (m2_ref, s2_ref, u2_ref))
     ):
@@ -407,38 +442,52 @@
             first = 0.9 * m_ref[at, :] + 0.1 * grad
             second = 0.999 * s_ref[at, :] + 0.001 * grad * grad
             u_ref[at, :] = first / first_bias / (jnp.sqrt(second / second_bias) + 1e-08)
-
-    for n in range(1, NF):
-        weight(0, n, fs).wait_send()
-        weight(1, n, fs).wait_send()
-        pltpu.make_async_remote_copy(
-            src_ref=Z.at[fs], dst_ref=Z.at[fs], send_sem=zs.at[n - 1], recv_sem=zr.at[n - 1],
-            device_id=(gy, gz, (fs + n) % NF), device_id_type=MESH,
-        ).wait_send()
-    for phase, buf in enumerate((X, H, E)):
-        halo_sent(buf, phase)
-    scattered(0, P1)
-    scattered(1, P2)
-    gather.wait_send()
+        stores[1 + k].start()
+        owed["store", 1 + k] = stores[1 + k].wait
+
+    finish()
+
+
+def hand_on(*refs):
+    sources, results, held, sems = refs[:3], refs[3:6], refs[6:9], refs[9]
+    inward = [
+        pltpu.make_async_copy(sources[n], held[n], sems.at[0, n]) for n in range(3)
+    ]
+    outward = [
+        pltpu.make_async_copy(held[n], results[n], sems.at[1, n]) for n in range(3)
+    ]
+    for copy in inward:
+        copy.start()
+    for n in range(3):
+        inward[n].wait()
+        outward[n].start()
+    for copy in outward:
+        copy.wait()
 
 
 def shards(
     coarse_field, fine_target, kernel_one, kernel_two,
     moment_one, moment_two, second_one, second_two,
 ):
-    vmem = pl.BlockSpec(memory_space=pltpu.VMEM)
+    hbm = pl.BlockSpec(memory_space=pltpu.HBM)
     dma = pltpu.SemaphoreType.DMA
     padded = pltpu.VMEM((TY + 2, TZ + 2, C, XL), bf16)
-    prediction, update_one, update_two = pl.pallas_call(
+    results = [
+        jax.ShapeDtypeStruct((C, TY, TZ, XL), bf16),
+        jax.ShapeDtypeStruct((C, COLS), f32),
+        jax.ShapeDtypeStruct((C, COLS), f32),
+    ]
+    computed = pl.pallas_call(
         kernel,
-        out_shape=[
-            jax.ShapeDtypeStruct((C, TY, TZ, XL), bf16),
-            jax.ShapeDtypeStruct((C, COLS), f32),
-            jax.ShapeDtypeStruct((C, COLS), f32),
-        ],
-        in_specs=[vmem] * 8,
-        out_specs=[vmem] * 3,
+        out_shape=results,
+        in_specs=[hbm] * 8,
+        out_specs=[hbm] * 3,
         scratch_shapes=[
+            pltpu.VMEM((C, TY, TZ, XL), bf16), pltpu.VMEM((C, TY, TZ, XL), bf16),
+        ] + [pltpu.VMEM((C, COLS), f32)] * 6 + [
+            pltpu.VMEM((C, TY, TZ, XL), bf16),
+            pltpu.VMEM((C, COLS), f32), pltpu.VMEM((C, COLS), f32),
+            dma((8,)), dma((3,)),
             padded, padded, padded,
             pltpu.VMEM((TY, TZ, C, XL), bf16),
             pltpu.VMEM((TY, TZ, C, XL), f32),
@@ -449,7 +498,6 @@
             pltpu.VMEM((C3, K9), bf16),
             pltpu.VMEM((C3, K9), bf16),
             pltpu.VMEM((C3, K9), bf16),
-            pltpu.VMEM((C3, K9), f32),
             pltpu.VMEM((16, NF, 8, 128), f32),
             pltpu.VMEM((16, NF, 8, 128), f32),
             pltpu.VMEM((PLANE, NF, 8, 128), f32),
@@ -464,12 +512,20 @@
             dma, dma,
         ],
         compiler_params=pltpu.CompilerParams(
-            collective_id=0, has_side_effects=True, vmem_limit_bytes=40 << 20
+            collective_id=0, has_side_effects=True, vmem_limit_bytes=60 << 20
         ),
     )(
         coarse_field[0], fine_target[0], kernel_one, kernel_two,
         moment_one, moment_two, second_one, second_two,
     )
+    prediction, update_one, update_two = pl.pallas_call(
+        hand_on,
+        out_shape=results,
+        in_specs=[hbm] * 3,
+        out_specs=[hbm] * 3,
+        scratch_shapes=[pltpu.VMEM(r.shape, r.dtype) for r in results] + [dma((2, 3))],
+        compiler_params=pltpu.CompilerParams(vmem_limit_bytes=60 << 20),
+    )(*computed)
     return prediction[None], update_one, update_two
 
 

time: 61.2 us -> 49.8 us (0.81)
  local copies, waits for them, and re-layouts: 9.3 us -> 0 us
  Pallas kernels: 50.8 us -> 49 us
    unnamed x19 -> x0, local copies, waits for them, and re-layouts: 9.3 us -> none
    pallas_call x1 -> x2, Pallas kernels: 50.8 us -> 49 us  [the longest x1 47.2 us: shards(): pl.pallas_call(kernel, out_shape=results, in_specs=[hbm] * 8, out_specs=[...]
where the time goes in v1:
time: 49.8 us; the launch traced here: 49.7 us
  Pallas kernels  49 us (98%)
  between operations  0.64 us (1%)
    pallas_call x1, Pallas kernels, shards(): pl.pallas_call(kernel, out_shape=results, in_specs=[hbm] * 8, out_specs=[...  47.2 us
    pallas_call x1, Pallas kernels, shards(): pl.pallas_call(hand_on, out_shape=results, in_specs=[hbm] * 3, out_specs=...  1.83 us

profile of v1, /device:TPU:1, one launch (start us, length us, event | category | flops | bytes accessed | tf_op | source)
XLA Modules:
  0.0 49.7 jit_solution(2421739286520073660)
XLA Ops:
  0.6 47.2 %shard_map.103 = (bf16[48,4,8,128]{3,2,1,0:T(8,128)(2,1)}, f32[48,324]{1,0:T(8,128)}, f32[48,324]{1,0:T(8,128)}) custom-call(bf16[48,4,8,128]{3,2,1,0:T(8,128)(2,1)} %bitcast.3, bf16[48,4,8,128]{3,2,1,0:T(8,128)(2,1)} %bitcast.4, f32[48,324]{1,0:T(8,128)} %k1_hbm.1, f32[48,324]{1,0:T(8,128)} %k2_hbm.1, f32[48,324]{1,0:T(8,128)} %m1_hbm.1, f32[48,324]{1,0:T(8,128)} %m2_hbm.1, ...), custom_call_target="tpu_custom_call" | custom-call | tf_op jit(solution)/shard_map/pallas_call | solution.py:480
  47.9 1.8 %shard_map.104 = (bf16[48,4,8,128]{3,2,1,0:T(8,128)(2,1)}, f32[48,324]{1,0:T(8,128)}, f32[48,324]{1,0:T(8,128)}) custom-call(bf16[48,4,8,128]{3,2,1,0:T(8,128)(2,1)} %get-tuple-element.9.refs_0_, f32[48,324]{1,0:T(8,128)} %get-tuple-element.10.refs_1_, f32[48,324]{1,0:T(8,128)} %get-tuple-element.11.refs_2_), custom_call_target="tpu_custom_call" | custom-call | tf_op jit(solution)/shard_map/pallas_call | solution.py:521

commit v2 on v1

--- a/solution.py
+++ b/solution.py
@@ -18,15 +18,15 @@
 C3 = 3 * C
 MESH = pl.DeviceIdType.MESH
 f32, bf16 = jnp.float32, jnp.bfloat16
-DIRS = [(0, -1), (0, 1), (-1, 0), (1, 0), (-1, -1), (-1, 1), (1, -1), (1, 1)]
-
-
-def edge(step, size, sending):
+DIRS = [(-1, -1), (-1, 1), (-1, 0), (1, -1), (1, 1), (1, 0), (0, -1), (0, 1)]
+
+
+def edge(step, size, width, sending):
     if step == 0:
-        return pl.ds(1, size)
+        return pl.ds(width, size)
     if sending:
-        return pl.ds(1 if step < 0 else size, 1)
-    return pl.ds(size + 1 if step < 0 else 0, 1)
+        return pl.ds(width if step < 0 else size, width)
+    return pl.ds(size + width if step < 0 else 0, width)
 
 
 def inside(value, count):
@@ -41,11 +41,12 @@
     return jnp.where(lane < XL - 1, pltpu.roll(v, XL - 1, 1), 0.0)
 
 
-def rows9(buf, cells):
+def rows9(buf, width, cells):
+    off = width - 1
     return jnp.concatenate(
         [
             jnp.concatenate(
-                [buf[y + dy, z:z + 3].reshape(C3, XL) for y, z in cells], 1
+                [buf[y + dy + off, z + off:z + off + 3].reshape(C3, XL) for y, z in cells], 1
             )
             for dy in range(3)
         ],
@@ -53,17 +54,18 @@
     )
 
 
-INNER = [((y, z), (y, z + 1)) for y in (1, 2) for z in (1, 3, 5)]
-RIM = [((y, z), (y, z + 1)) for y in (0, 3) for z in (0, 2, 4, 6)]
-RIM += [((y, 0), (y, TZ - 1)) for y in (1, 2)]
+LOW = [((0, z), (0, z + 1)) for z in range(0, TZ, 2)]
+HIGH = [((TY - 1, z), (TY - 1, z + 1)) for z in range(0, TZ, 2)]
+SIDES = [((y, 0), (y, TZ - 1)) for y in range(1, TY - 1)]
+INNER = [((y, z), (y, z + 1)) for y in range(1, TY - 1) for z in range(1, TZ - 1, 2)]
+WIDE = [((y, z), (y, z + 1)) for y in range(-1, TY + 1) for z in range(-1, TZ + 1, 2)]
 PLANES = [tuple((y, z) for z in range(TZ)) for y in range(TY)]
 
 
 def kernel(
     x_hbm, t_hbm, k1_hbm, k2_hbm, m1_hbm, m2_hbm, s1_hbm, s2_hbm,
-    pred_hbm, u1_hbm, u2_hbm,
-    x_ref, t_ref, k1_ref, k2_ref, m1_ref, m2_ref, s1_ref, s2_ref,
-    pred_ref, u1_ref, u2_ref, ls, os, X, H, E, E1, A1, TG, TS, PS, WG, W1, W2, WB, P1, P2, R, Z, TT, Q, A,
+    pred_ref, u1_ref, u2_ref,
+    x_ref, t_ref, k1_ref, k2_ref, m1_ref, m2_ref, s1_ref, s2_ref, ls, X, H, E, E1, A1, TG, TS, PS, WG, W1, W2, WB, P1, P2, R, Z, TT, Q, A,
     hs, hr, ws, wr, gs, gr, zs, zr, qs, qr,
 ):
     gy = lax.axis_index("gy")
@@ -93,13 +95,6 @@
     for n, load in enumerate(loads):
         load.start()
         owed["load", n] = load.wait
-    stores = [
-        pltpu.make_async_copy(ref, result, os.at[n])
-        for n, (ref, result) in enumerate((
-            (pred_ref, pred_hbm), (u1_ref, u1_hbm), (u2_ref, u2_hbm)
-        ))
-    ]
-
     def plane_device(index):
         return (index // GZ, index % GZ, fs)
 
@@ -125,7 +120,7 @@
     for y in range(TY):
         TS[y] = x_ref[:, y].astype(f32).reshape(C * TZ, XL)
         for z in range(TZ):
-            X[y + 1, z + 1] = TS[y, pl.ds(z, C, stride=TZ), :].astype(bf16)
+            X[y + 2, z + 2] = TS[y, pl.ds(z, C, stride=TZ), :].astype(bf16)
 
     send_ok = [
         jnp.logical_and(inside(gy + dy, GY), inside(gz + dz, GZ)) for dy, dz in DIRS
@@ -134,20 +129,21 @@
         jnp.logical_and(inside(gy - dy, GY), inside(gz - dz, GZ)) for dy, dz in DIRS
     ]
 
-    for d, (dy, dz) in enumerate(DIRS):
-        at = (edge(dy, TY, False), edge(dz, TZ, False))
-
-        @pl.when(jnp.logical_not(recv_ok[d]))
-        def _():
-            for buf in (X, H, E):
-                region = buf.at[at]
+    def clear_outside(buf, width):
+        for d, (dy, dz) in enumerate(DIRS):
+            @pl.when(jnp.logical_not(recv_ok[d]))
+            def _():
+                region = buf.at[edge(dy, TY, width, False), edge(dz, TZ, width, False)]
                 region[...] = jnp.zeros(region.shape, bf16)
 
-    def halo(buf, phase, d):
+    clear_outside(X, 2)
+    clear_outside(E, 1)
+
+    def halo(buf, width, phase, d):
         dy, dz = DIRS[d]
         return pltpu.make_async_remote_copy(
-            src_ref=buf.at[edge(dy, TY, True), edge(dz, TZ, True)],
-            dst_ref=buf.at[edge(dy, TY, False), edge(dz, TZ, False)],
+            src_ref=buf.at[edge(dy, TY, width, True), edge(dz, TZ, width, True)],
+            dst_ref=buf.at[edge(dy, TY, width, False), edge(dz, TZ, width, False)],
             send_sem=hs.at[phase, d],
             recv_sem=hr.at[phase, d],
             device_id=(
@@ -156,23 +152,23 @@
             device_id_type=MESH,
         )
 
-    def halo_start(buf, phase):
+    def halo_start(buf, width, phase, dirs=range(8)):
         def arrived():
             for d in range(8):
                 @pl.when(recv_ok[d])
                 def _():
-                    halo(buf, phase, d).wait_recv()
+                    halo(buf, width, phase, d).wait_recv()
 
         def sent():
             for d in range(8):
                 @pl.when(send_ok[d])
                 def _():
-                    halo(buf, phase, d).wait_send()
-
-        for d in range(8):
+                    halo(buf, width, phase, d).wait_send()
+
+        for d in dirs:
             @pl.when(send_ok[d])
             def _():
-                halo(buf, phase, d).start()
+                halo(buf, width, phase, d).start()
         owed["halo", phase], owed["halo sent", phase] = arrived, sent
 
     def weight(k, n, owner):
@@ -201,7 +197,7 @@
     pl.semaphore_wait(barrier, PLANE - 1 + NF - 1)
 
     weight_start(0)
-    halo_start(X, 0)
+    halo_start(X, 2, 0)
     weight_start(1)
 
     settle(("load", 3))
@@ -222,8 +218,8 @@
     settle(("weight", 0))
     forward_matrix(gathered(0), W1)
 
-    def conv(w, buf, cells, back=False):
-        out = jnp.dot(w[...], rows9(buf, cells), preferred_element_type=f32)
+    def conv(w, buf, width, cells, back=False):
+        out = jnp.dot(w[...], rows9(buf, width, cells), preferred_element_type=f32)
         res = []
         for h in range(len(cells)):
             q = out[:, h * XL:(h + 1) * XL]
@@ -233,16 +229,13 @@
             res.append(mid + roll_right(low, lane) + roll_left(high, lane))
         return zip(cells, res)
 
-    def conv1(groups):
-        for cells in groups:
-            for (y, z), a1 in conv(W1, X, cells):
+    settle(("halo", 0))
+    for cells in WIDE:
+        for (y, z), a1 in conv(W1, X, 2, cells):
+            if 0 <= y < TY and 0 <= z < TZ:
                 A1[y, z] = a1
-                H[y + 1, z + 1] = jnp.maximum(a1, 0.0).astype(bf16)
-
-    settle(("halo", 0))
-    conv1(RIM)
-    halo_start(H, 1)
-    conv1(INNER)
+            H[y + 1, z + 1] = jnp.maximum(a1, 0.0).astype(bf16)
+    clear_outside(H, 1)
 
     settle(("weight", 1))
     full2 = gathered(1)
@@ -250,15 +243,18 @@
 
     def conv2(groups):
         for cells in groups:
-            for (y, z), a2 in conv(W2, H, cells):
-                total = X[y + 1, z + 1].astype(f32) + a2
+            for (y, z), a2 in conv(W2, H, 1, cells):
+                total = X[y + 2, z + 2].astype(f32) + a2
                 PS[y, pl.ds(z, C, stride=TZ), :] = total
                 E[y + 1, z + 1] = (total - TG[y, z]).astype(bf16)
 
+    conv2(LOW)
+    halo_start(E, 1, 1, (0, 1, 2))
+    conv2(HIGH)
+    halo_start(E, 1, 1, (3, 4, 5))
+    conv2(SIDES)
+    halo_start(E, 1, 1, (6, 7))
     conv2(INNER)
-    settle(("halo", 1))
-    conv2(RIM)
-    halo_start(E, 2)
 
     def shifted(e):
         v = e.astype(f32)
@@ -266,12 +262,12 @@
             [roll_left(v, lane).astype(bf16), e, roll_right(v, lane).astype(bf16)], 0
         )
 
-    def weight_grad(buf, err):
+    def weight_grad(buf, width, err):
         grad = jnp.zeros((K9, C3), f32)
         for cells in PLANES:
             right = jnp.concatenate([shifted(err(y, z)) for y, z in cells], 1)
             grad += lax.dot_general(
-                rows9(buf, cells), right, (((1,), (1,)), ((), ())),
+                rows9(buf, width, cells), right, (((1,), (1,)), ((), ())),
                 preferred_element_type=f32,
             )
         return grad.T
@@ -340,7 +336,7 @@
 
         owed["parts", k], owed["scatter sent", k] = parts, sent
 
-    grad2 = weight_grad(H, lambda y, z: E[y + 1, z + 1])
+    grad2 = weight_grad(H, 1, lambda y, z: E[y + 1, z + 1])
     pack(grad2, P2)
     scatter(1, P2)
 
@@ -356,20 +352,18 @@
 
     def back(groups):
         for cells in groups:
-            for (y, z), b in conv(WB, E, cells, True):
+            for (y, z), b in conv(WB, E, 1, cells, True):
                 E1[y, z] = jnp.where(A1[y, z] > 0, b, 0.0).astype(bf16)
 
     back(INNER)
-    settle(("halo", 2))
-    back(RIM)
-    grad1 = weight_grad(X, lambda y, z: E1[y, z])
+    settle(("halo", 1))
+    back(LOW + HIGH + SIDES)
+    grad1 = weight_grad(X, 2, lambda y, z: E1[y, z])
     pack(grad1, P1)
     scatter(0, P1)
 
     for y in range(TY):
         pred_ref[:, y] = PS[y].reshape(C, TZ, XL).astype(bf16)
-    stores[0].start()
-    owed["store", 0] = stores[0].wait
 
     settle(("parts", 1))
     settle(("parts", 0))
@@ -442,26 +436,17 @@
             first = 0.9 * m_ref[at, :] + 0.1 * grad
             second = 0.999 * s_ref[at, :] + 0.001 * grad * grad
             u_ref[at, :] = first / first_bias / (jnp.sqrt(second / second_bias) + 1e-08)
-        stores[1 + k].start()
-        owed["store", 1 + k] = stores[1 + k].wait
 
     finish()
 
 
 def hand_on(*refs):
-    sources, results, held, sems = refs[:3], refs[3:6], refs[6:9], refs[9]
-    inward = [
-        pltpu.make_async_copy(sources[n], held[n], sems.at[0, n]) for n in range(3)
+    copies = [
+        pltpu.make_async_copy(refs[n], refs[3 + n], refs[6].at[n]) for n in range(3)
     ]
-    outward = [
-        pltpu.make_async_copy(held[n], results[n], sems.at[1, n]) for n in range(3)
-    ]
-    for copy in inward:
+    for copy in copies:
         copy.start()
-    for n in range(3):
-        inward[n].wait()
-        outward[n].start()
-    for copy in outward:
+    for copy in copies:
         copy.wait()
 
 
@@ -470,8 +455,9 @@
     moment_one, moment_two, second_one, second_two,
 ):
     hbm = pl.BlockSpec(memory_space=pltpu.HBM)
+    vmem = pl.BlockSpec(memory_space=pltpu.VMEM)
     dma = pltpu.SemaphoreType.DMA
-    padded = pltpu.VMEM((TY + 2, TZ + 2, C, XL), bf16)
+    padded = [pltpu.VMEM((TY + 2 * w, TZ + 2 * w, C, XL), bf16) for w in (2, 1, 1)]
     results = [
         jax.ShapeDtypeStruct((C, TY, TZ, XL), bf16),
         jax.ShapeDtypeStruct((C, COLS), f32),
@@ -479,16 +465,14 @@
     ]
     computed = pl.pallas_call(
         kernel,
-        out_shape=results,
+        out_shape=[pltpu.VMEM(r.shape, r.dtype) for r in results],
         in_specs=[hbm] * 8,
-        out_specs=[hbm] * 3,
+        out_specs=[vmem] * 3,
         scratch_shapes=[
             pltpu.VMEM((C, TY, TZ, XL), bf16), pltpu.VMEM((C, TY, TZ, XL), bf16),
         ] + [pltpu.VMEM((C, COLS), f32)] * 6 + [
-            pltpu.VMEM((C, TY, TZ, XL), bf16),
-            pltpu.VMEM((C, COLS), f32), pltpu.VMEM((C, COLS), f32),
-            dma((8,)), dma((3,)),
-            padded, padded, padded,
+            dma((8,)),
+            *padded,
             pltpu.VMEM((TY, TZ, C, XL), bf16),
             pltpu.VMEM((TY, TZ, C, XL), f32),
             pltpu.VMEM((TY, TZ, C, XL), f32),
@@ -505,7 +489,7 @@
             pltpu.VMEM((NF, 8, 128), f32),
             pltpu.VMEM((2, 8, 128), f32),
             pltpu.VMEM((PLANE, 2, 8, 128), f32),
-            dma((3, 8)), dma((3, 8)),
+            dma((2, 8)), dma((2, 8)),
             dma((2, 3)), dma((2, 3)),
             dma((2,)), dma,
             dma((3,)), dma((3,)),
@@ -521,10 +505,10 @@
     prediction, update_one, update_two = pl.pallas_call(
         hand_on,
         out_shape=results,
-        in_specs=[hbm] * 3,
+        in_specs=[vmem] * 3,
         out_specs=[hbm] * 3,
-        scratch_shapes=[pltpu.VMEM(r.shape, r.dtype) for r in results] + [dma((2, 3))],
-        compiler_params=pltpu.CompilerParams(vmem_limit_bytes=60 << 20),
+        scratch_shapes=[dma((3,))],
+        compiler_params=pltpu.CompilerParams(vmem_limit_bytes=4 << 20),
     )(*computed)
     return prediction[None], update_one, update_two
 

time: 49.8 us -> 46.1 us (0.926)
  Pallas kernels: 49 us -> 45 us
    pallas_call x2, Pallas kernels: 49 us -> 45 us  [the longest x1 44.2 us: shards(): pl.pallas_call(kernel, out_shape=[pltpu.VMEM(r.shape, r.dtype) for r in r...]
where the time goes in v2:
time: 46.1 us; the launch traced here: 45.6 us
  Pallas kernels  45 us (98%)
  between operations  0.64 us (1%)
    pallas_call x1, Pallas kernels, shards(): pl.pallas_call(kernel, out_shape=[pltpu.VMEM(r.shape, r.dtype) for r in r...  44.2 us

profile of v2, /device:TPU:1, one launch (start us, length us, event | category | flops | bytes accessed | tf_op | source)
XLA Modules:
  0.0 45.6 jit_solution(14950822473714074199)
XLA Ops:
  0.6 44.2 %shard_map.103 = (bf16[48,4,8,128]{3,2,1,0:T(8,128)(2,1)S(1)}, f32[48,324]{1,0:T(8,128)S(1)}, f32[48,324]{1,0:T(8,128)S(1)}) custom-call(bf16[48,4,8,128]{3,2,1,0:T(8,128)(2,1)} %bitcast.3, bf16[48,4,8,128]{3,2,1,0:T(8,128)(2,1)} %bitcast.4, f32[48,324]{1,0:T(8,128)} %k1_hbm.1, f32[48,324]{1,0:T(8,128)} %k2_hbm.1, f32[48,324]{1,0:T(8,128)} %m1_hbm.1, ...), custom_call_target="tpu_custom_call" | custom-call | tf_op jit(solution)/shard_map/pallas_call | solution.py:466
  44.8 0.8 %shard_map.104 = (bf16[48,4,8,128]{3,2,1,0:T(8,128)(2,1)}, f32[48,324]{1,0:T(8,128)}, f32[48,324]{1,0:T(8,128)}) custom-call(bf16[48,4,8,128]{3,2,1,0:T(8,128)(2,1)S(1)} %get-tuple-element.9.refs_0_, f32[48,324]{1,0:T(8,128)S(1)} %get-tuple-element.10.refs_1_, f32[48,324]{1,0:T(8,128)S(1)} %get-tuple-element.11.refs_2_), custom_call_target="tpu_custom_call" | custom-call | tf_op jit(solution)/shard_map/pallas_call | solution.py:505

commit v3 on v2

--- a/solution.py
+++ b/solution.py
@@ -273,6 +273,7 @@
         return grad.T
 
     def pack(grad, out):
+        shares = []
         for f in range(NF):
             pieces = []
             for third in range(3):
@@ -288,8 +289,10 @@
                     col += width
             pieces.append(jnp.zeros((16, 1024 - 3 * COLS), f32))
             flat = jnp.concatenate(pieces, 1)
-            for t in range(16):
-                out[t, f] = flat[(t // 8) * 8:(t // 8) * 8 + 8, (t % 8) * 128:(t % 8 + 1) * 128]
+            shares.append(flat)
+        for t in range(16):
+            at = (slice((t // 8) * 8, (t // 8) * 8 + 8), slice((t % 8) * 128, (t % 8 + 1) * 128))
+            out[t] = jnp.concatenate([flat[at] for flat in shares], 0).astype(bf16)
 
     def scatter(k, src):
         def send(n, carry):
@@ -367,10 +370,10 @@
 
     settle(("parts", 1))
     settle(("parts", 0))
-    own = R[0]
+    own = R[0].astype(f32)
     for n in range(1, PLANE):
-        own = own + R[n]
-    Z[fs] = own
+        own = own + R[n].astype(f32)
+    Z[fs] = own.reshape(NF, 8, 128)
 
     def along(n, owner):
         return pltpu.make_async_remote_copy(
@@ -392,8 +395,11 @@
     settle("sums")
     total = Z[0] + Z[1] + Z[2] + Z[3]
     TT[...] = total
-    Q[0] = TT[fs]
-    Q[1] = jnp.sum(total * total, 0)
+    squares = jnp.sum(jnp.sum(total * total, 0), 0, keepdims=True)
+    rounded = squares.astype(bf16).astype(f32)
+    Q[...] = jnp.concatenate(
+        [TT[fs], rounded, squares - rounded, jnp.zeros((6, 128), f32)], 0
+    ).astype(bf16)
 
     slot = core * 16 + tile
     A[slot] = Q[...]
@@ -413,9 +419,10 @@
     owed["gather"], owed["gather sent"] = gather.wait_recv, gather.wait_send
     settle("gather")
 
-    squares = A[0, 1]
-    for n in range(1, PLANE):
-        squares = squares + A[n, 1]
+    tiles = [A[n].astype(f32) for n in range(PLANE)]
+    squares = tiles[0][8:]
+    for tile_in in tiles[1:]:
+        squares = squares + tile_in[8:]
     norm = jnp.sqrt(jnp.sum(squares, keepdims=True))
     factor = jnp.minimum(1.0, 1.0 / (norm + 1e-06))
     for n in range(4, 8):
@@ -425,7 +432,7 @@
     ):
         flat = jnp.concatenate(
             [
-                jnp.concatenate([A[k * 16 + r * 8 + t, 0] for t in range(8)], 1)
+                jnp.concatenate([tiles[k * 16 + r * 8 + t][:8] for t in range(8)], 1)
                 for r in range(2)
             ],
             0,
@@ -482,13 +489,13 @@
             pltpu.VMEM((C3, K9), bf16),
             pltpu.VMEM((C3, K9), bf16),
             pltpu.VMEM((C3, K9), bf16),
-            pltpu.VMEM((16, NF, 8, 128), f32),
-            pltpu.VMEM((16, NF, 8, 128), f32),
-            pltpu.VMEM((PLANE, NF, 8, 128), f32),
+            pltpu.VMEM((16, NF * 8, 128), bf16),
+            pltpu.VMEM((16, NF * 8, 128), bf16),
+            pltpu.VMEM((PLANE, NF * 8, 128), bf16),
             pltpu.VMEM((NF, NF, 8, 128), f32),
             pltpu.VMEM((NF, 8, 128), f32),
-            pltpu.VMEM((2, 8, 128), f32),
-            pltpu.VMEM((PLANE, 2, 8, 128), f32),
+            pltpu.VMEM((16, 128), bf16),
+            pltpu.VMEM((PLANE, 16, 128), bf16),
             dma((2, 8)), dma((2, 8)),
             dma((2, 3)), dma((2, 3)),
             dma((2,)), dma,

time: 46.1 us -> 43.4 us (0.941)
  Pallas kernels: 45 us -> 42.7 us
    pallas_call x1, Pallas kernels: 44.2 us -> 41.9 us  [shards(): pl.pallas_call(kernel, out_shape=[pltpu.VMEM(r.shape, r.dtype) for r in r...]
where the time goes in v3:
time: 43.4 us; the launch traced here: 43.3 us
  Pallas kernels  42.7 us (98%)
  between operations  0.64 us (1%)
    pallas_call x1, Pallas kernels, shards(): pl.pallas_call(kernel, out_shape=[pltpu.VMEM(r.shape, r.dtype) for r in r...  41.9 us

profile of v3, /device:TPU:1, one launch (start us, length us, event | category | flops | bytes accessed | tf_op | source)
XLA Modules:
  0.0 43.3 jit_solution(18067720195698859103)
XLA Ops:
  0.6 41.9 %shard_map.103 = (bf16[48,4,8,128]{3,2,1,0:T(8,128)(2,1)S(1)}, f32[48,324]{1,0:T(8,128)S(1)}, f32[48,324]{1,0:T(8,128)S(1)}) custom-call(bf16[48,4,8,128]{3,2,1,0:T(8,128)(2,1)} %bitcast.3, bf16[48,4,8,128]{3,2,1,0:T(8,128)(2,1)} %bitcast.4, f32[48,324]{1,0:T(8,128)} %k1_hbm.1, f32[48,324]{1,0:T(8,128)} %k2_hbm.1, f32[48,324]{1,0:T(8,128)} %m1_hbm.1, ...), custom_call_target="tpu_custom_call" | custom-call | tf_op jit(solution)/shard_map/pallas_call | solution.py:473
  42.5 0.8 %shard_map.104 = (bf16[48,4,8,128]{3,2,1,0:T(8,128)(2,1)}, f32[48,324]{1,0:T(8,128)}, f32[48,324]{1,0:T(8,128)}) custom-call(bf16[48,4,8,128]{3,2,1,0:T(8,128)(2,1)S(1)} %get-tuple-element.9.refs_0_, f32[48,324]{1,0:T(8,128)S(1)} %get-tuple-element.10.refs_1_, f32[48,324]{1,0:T(8,128)S(1)} %get-tuple-element.11.refs_2_), custom_call_target="tpu_custom_call" | custom-call | tf_op jit(solution)/shard_map/pallas_call | solution.py:512

commit v4 on v3

--- a/solution.py
+++ b/solution.py
@@ -58,14 +58,15 @@
 HIGH = [((TY - 1, z), (TY - 1, z + 1)) for z in range(0, TZ, 2)]
 SIDES = [((y, 0), (y, TZ - 1)) for y in range(1, TY - 1)]
 INNER = [((y, z), (y, z + 1)) for y in range(1, TY - 1) for z in range(1, TZ - 1, 2)]
-WIDE = [((y, z), (y, z + 1)) for y in range(-1, TY + 1) for z in range(-1, TZ + 1, 2)]
+WIDE = [((y, z), (y, z + 1)) for y in (-1, 0, TY - 1, TY) for z in range(-1, TZ + 1, 2)]
+WIDE += [((y, z), (y, z + 1)) for y in range(1, TY - 1) for z in (-1, TZ - 1)]
 PLANES = [tuple((y, z) for z in range(TZ)) for y in range(TY)]
 
 
 def kernel(
     x_hbm, t_hbm, k1_hbm, k2_hbm, m1_hbm, m2_hbm, s1_hbm, s2_hbm,
     pred_ref, u1_ref, u2_ref,
-    x_ref, t_ref, k1_ref, k2_ref, m1_ref, m2_ref, s1_ref, s2_ref, ls, X, H, E, E1, A1, TG, TS, PS, WG, W1, W2, WB, P1, P2, R, Z, TT, Q, A,
+    x_ref, t_ref, k1_ref, k2_ref, m1_ref, m2_ref, s1_ref, s2_ref, ls, X, H, E, E1, A1, TG, TS, PS, WG, W1, W2, WB, G, P1, P2, R, Z, TT, Q, A,
     hs, hr, ws, wr, gs, gr, zs, zr, qs, qr,
 ):
     gy = lax.axis_index("gy")
@@ -229,17 +230,20 @@
             res.append(mid + roll_right(low, lane) + roll_left(high, lane))
         return zip(cells, res)
 
-    settle(("halo", 0))
-    for cells in WIDE:
-        for (y, z), a1 in conv(W1, X, 2, cells):
-            if 0 <= y < TY and 0 <= z < TZ:
-                A1[y, z] = a1
-            H[y + 1, z + 1] = jnp.maximum(a1, 0.0).astype(bf16)
-    clear_outside(H, 1)
-
+    def conv1(groups):
+        for cells in groups:
+            for (y, z), a1 in conv(W1, X, 2, cells):
+                if 0 <= y < TY and 0 <= z < TZ:
+                    A1[y, z] = a1
+                H[y + 1, z + 1] = jnp.maximum(a1, 0.0).astype(bf16)
+
+    conv1(INNER)
     settle(("weight", 1))
     full2 = gathered(1)
     forward_matrix(full2, W2)
+    settle(("halo", 0))
+    conv1(WIDE)
+    clear_outside(H, 1)
 
     def conv2(groups):
         for cells in groups:
@@ -262,17 +266,19 @@
             [roll_left(v, lane).astype(bf16), e, roll_right(v, lane).astype(bf16)], 0
         )
 
-    def weight_grad(buf, width, err):
-        grad = jnp.zeros((K9, C3), f32)
-        for cells in PLANES:
+    def weight_grad(buf, width, err, groups):
+        grad = None
+        for cells in groups:
             right = jnp.concatenate([shifted(err(y, z)) for y, z in cells], 1)
-            grad += lax.dot_general(
+            part = lax.dot_general(
                 rows9(buf, width, cells), right, (((1,), (1,)), ((), ())),
                 preferred_element_type=f32,
             )
-        return grad.T
+            grad = part if grad is None else grad + part
+        return grad
 
     def pack(grad, out):
+        grad = grad.T
         shares = []
         for f in range(NF):
             pieces = []
@@ -339,7 +345,7 @@
 
         owed["parts", k], owed["scatter sent", k] = parts, sent
 
-    grad2 = weight_grad(H, 1, lambda y, z: E[y + 1, z + 1])
+    grad2 = weight_grad(H, 1, lambda y, z: E[y + 1, z + 1], PLANES)
     pack(grad2, P2)
     scatter(1, P2)
 
@@ -358,10 +364,15 @@
             for (y, z), b in conv(WB, E, 1, cells, True):
                 E1[y, z] = jnp.where(A1[y, z] > 0, b, 0.0).astype(bf16)
 
+    def own_error(y, z):
+        return E1[y, z]
+
     back(INNER)
+    G[...] = weight_grad(X, 2, own_error, [sum(INNER, ())])
     settle(("halo", 1))
-    back(LOW + HIGH + SIDES)
-    grad1 = weight_grad(X, 2, lambda y, z: E1[y, z])
+    rim = LOW + HIGH + SIDES
+    back(rim)
+    grad1 = G[...] + weight_grad(X, 2, own_error, [sum(rim[:5], ()), sum(rim[5:], ())])
     pack(grad1, P1)
     scatter(0, P1)
 
@@ -489,6 +500,7 @@
             pltpu.VMEM((C3, K9), bf16),
             pltpu.VMEM((C3, K9), bf16),
             pltpu.VMEM((C3, K9), bf16),
+            pltpu.VMEM((K9, C3), f32),
             pltpu.VMEM((16, NF * 8, 128), bf16),
             pltpu.VMEM((16, NF * 8, 128), bf16),
             pltpu.VMEM((PLANE, NF * 8, 128), bf16),

time: 43.4 us -> 42.9 us (0.988)
  Pallas kernels: 42.7 us -> 42.1 us
    pallas_call x1, Pallas kernels: 41.9 us -> 41.3 us  [shards(): pl.pallas_call(kernel, out_shape=[pltpu.VMEM(r.shape, r.dtype) for r in r...]
where the time goes in v4:
time: 42.9 us; the launch traced here: 42.7 us
  Pallas kernels  42.1 us (98%)
  between operations  0.64 us (1%)
    pallas_call x1, Pallas kernels, shards(): pl.pallas_call(kernel, out_shape=[pltpu.VMEM(r.shape, r.dtype) for r in r...  41.3 us

profile of v4, /device:TPU:1, one launch (start us, length us, event | category | flops | bytes accessed | tf_op | source)
XLA Modules:
  0.0 42.7 jit_solution(1782716703966354770)
XLA Ops:
  0.6 41.3 %shard_map.103 = (bf16[48,4,8,128]{3,2,1,0:T(8,128)(2,1)S(1)}, f32[48,324]{1,0:T(8,128)S(1)}, f32[48,324]{1,0:T(8,128)S(1)}) custom-call(bf16[48,4,8,128]{3,2,1,0:T(8,128)(2,1)} %bitcast.3, bf16[48,4,8,128]{3,2,1,0:T(8,128)(2,1)} %bitcast.4, f32[48,324]{1,0:T(8,128)} %k1_hbm.1, f32[48,324]{1,0:T(8,128)} %k2_hbm.1, f32[48,324]{1,0:T(8,128)} %m1_hbm.1, ...), custom_call_target="tpu_custom_call" | custom-call | tf_op jit(solution)/shard_map/pallas_call | solution.py:484
  41.9 0.8 %shard_map.104 = (bf16[48,4,8,128]{3,2,1,0:T(8,128)(2,1)}, f32[48,324]{1,0:T(8,128)}, f32[48,324]{1,0:T(8,128)}) custom-call(bf16[48,4,8,128]{3,2,1,0:T(8,128)(2,1)S(1)} %get-tuple-element.9.refs_0_, f32[48,324]{1,0:T(8,128)S(1)} %get-tuple-element.10.refs_1_, f32[48,324]{1,0:T(8,128)S(1)} %get-tuple-element.11.refs_2_), custom_call_target="tpu_custom_call" | custom-call | tf_op jit(solution)/shard_map/pallas_call | solution.py:524

commit v5 on v4

--- a/solution.py
+++ b/solution.py
@@ -54,12 +54,14 @@
     )
 
 
+DOWN, UP, ACROSS = (0, 1, 2), (3, 4, 5), (6, 7)
+CORNERS = (0, 1, 3, 4)
 LOW = [((0, z), (0, z + 1)) for z in range(0, TZ, 2)]
 HIGH = [((TY - 1, z), (TY - 1, z + 1)) for z in range(0, TZ, 2)]
 SIDES = [((y, 0), (y, TZ - 1)) for y in range(1, TY - 1)]
 INNER = [((y, z), (y, z + 1)) for y in range(1, TY - 1) for z in range(1, TZ - 1, 2)]
 WIDE = [((y, z), (y, z + 1)) for y in (-1, 0, TY - 1, TY) for z in range(-1, TZ + 1, 2)]
-WIDE += [((y, z), (y, z + 1)) for y in range(1, TY - 1) for z in (-1, TZ - 1)]
+WIDE_Z = [((y, z), (y, z + 1)) for y in range(1, TY - 1) for z in (-1, TZ - 1)]
 PLANES = [tuple((y, z) for z in range(TZ)) for y in range(TY)]
 
 
@@ -73,8 +75,8 @@
     gz = lax.axis_index("gz")
     fs = lax.axis_index("fsdp")
     core = gy % 2
-    place = gy * GZ + gz
-    tile = (gy // 2) * GZ + gz
+    half = gy // 2
+    tile = half * GZ + gz
     lane = lax.broadcasted_iota(jnp.int32, (C, XL), 1)
 
     loads = [
@@ -96,21 +98,24 @@
     for n, load in enumerate(loads):
         load.start()
         owed["load", n] = load.wait
-    def plane_device(index):
-        return (index // GZ, index % GZ, fs)
-
     barrier = pltpu.get_barrier_semaphore()
 
-    def greet(n, carry):
+    def further(at, size):
+        out = [at]
+        for _ in range(1, size):
+            out.append(jnp.where(out[-1] == size - 1, 0, out[-1] + 1))
+        return out
+
+    ys, zs_at, fs_at = further(gy, GY), further(gz, GZ), further(fs, NF)
+    others = [(a, b) for b in range(GZ) for a in range(GY)][1:]
+
+    for a, b in others:
         pl.semaphore_signal(
-            barrier, inc=1, device_id=plane_device((place + n) % PLANE), device_id_type=MESH
-        )
-        return carry
-
-    lax.fori_loop(1, PLANE, greet, 0)
+            barrier, inc=1, device_id=(ys[a], zs_at[b], fs), device_id_type=MESH
+        )
     for n in range(1, NF):
         pl.semaphore_signal(
-            barrier, inc=1, device_id=(gy, gz, (fs + n) % NF), device_id_type=MESH
+            barrier, inc=1, device_id=(gy, gz, fs_at[n]), device_id_type=MESH
         )
 
     for k, ref in enumerate((k1_ref, k2_ref)):
@@ -140,37 +145,66 @@
     clear_outside(X, 2)
     clear_outside(E, 1)
 
-    def halo(buf, width, phase, d):
+    def halo(buf, width, phase, d, relay=False):
         dy, dz = DIRS[d]
         return pltpu.make_async_remote_copy(
-            src_ref=buf.at[edge(dy, TY, width, True), edge(dz, TZ, width, True)],
+            src_ref=buf.at[edge(dy, TY, width, True), edge(dz, TZ, width, not relay)],
             dst_ref=buf.at[edge(dy, TY, width, False), edge(dz, TZ, width, False)],
             send_sem=hs.at[phase, d],
             recv_sem=hr.at[phase, d],
             device_id=(
-                jnp.clip(gy + dy, 0, GY - 1), jnp.clip(gz + dz, 0, GZ - 1), fs
+                jnp.clip(gy + dy, 0, GY - 1),
+                gz if relay else jnp.clip(gz + dz, 0, GZ - 1),
+                fs,
             ),
             device_id_type=MESH,
         )
 
-    def halo_start(buf, width, phase, dirs=range(8)):
-        def arrived():
-            for d in range(8):
+    def halo_start(buf, width, phase, dirs, relay=False):
+        def owe(d):
+            def arrived():
                 @pl.when(recv_ok[d])
                 def _():
                     halo(buf, width, phase, d).wait_recv()
 
-        def sent():
-            for d in range(8):
+            def sent():
                 @pl.when(send_ok[d])
                 def _():
                     halo(buf, width, phase, d).wait_send()
 
+            owed["halo", phase, d], owed["halo sent", phase, d] = arrived, sent
+
         for d in dirs:
-            @pl.when(send_ok[d])
+            direct = send_ok[d]
+            if relay and d in CORNERS:
+                direct = jnp.logical_and(direct, core == (0 if DIRS[d][0] < 0 else 1))
+
+            @pl.when(direct)
             def _():
                 halo(buf, width, phase, d).start()
-        owed["halo", phase], owed["halo sent", phase] = arrived, sent
+            owe(d)
+
+    def relay_start(buf, width, phase):
+        for d in CORNERS:
+            dy, dz = DIRS[d]
+            passing = jnp.logical_and(inside(gz - dz, GZ), core == (1 if dy < 0 else 0))
+
+            @pl.when(passing)
+            def _():
+                halo(buf, width, phase, d, True).start()
+
+            def sent(d=d, dy=dy, passing=passing):
+                direct = jnp.logical_and(send_ok[d], core == (0 if dy < 0 else 1))
+
+                @pl.when(jnp.logical_or(direct, passing))
+                def _():
+                    halo(buf, width, phase, d).wait_send()
+
+            owed["halo sent", phase, d] = sent
+
+    def halo_settle(phase, dirs):
+        for d in dirs:
+            settle(("halo", phase, d))
 
     def weight(k, n, owner):
         return pltpu.make_async_remote_copy(
@@ -178,14 +212,14 @@
             dst_ref=WG.at[k, owner],
             send_sem=ws.at[k, n - 1],
             recv_sem=wr.at[k, n - 1],
-            device_id=(gy, gz, (fs + n) % NF),
+            device_id=(gy, gz, fs_at[n]),
             device_id_type=MESH,
         )
 
     def weight_start(k):
         def arrived():
             for n in range(1, NF):
-                weight(k, n, (fs - n + NF) % NF).wait_recv()
+                weight(k, n, fs_at[NF - n]).wait_recv()
 
         def sent():
             for n in range(1, NF):
@@ -198,7 +232,7 @@
     pl.semaphore_wait(barrier, PLANE - 1 + NF - 1)
 
     weight_start(0)
-    halo_start(X, 2, 0)
+    halo_start(X, 2, 0, range(8), True)
     weight_start(1)
 
     settle(("load", 3))
@@ -238,10 +272,13 @@
                 H[y + 1, z + 1] = jnp.maximum(a1, 0.0).astype(bf16)
 
     conv1(INNER)
+    halo_settle(0, ACROSS)
+    relay_start(X, 2, 0)
     settle(("weight", 1))
     full2 = gathered(1)
     forward_matrix(full2, W2)
-    settle(("halo", 0))
+    conv1(WIDE_Z)
+    halo_settle(0, DOWN + UP)
     conv1(WIDE)
     clear_outside(H, 1)
 
@@ -253,11 +290,11 @@
                 E[y + 1, z + 1] = (total - TG[y, z]).astype(bf16)
 
     conv2(LOW)
-    halo_start(E, 1, 1, (0, 1, 2))
+    halo_start(E, 1, 1, DOWN)
     conv2(HIGH)
-    halo_start(E, 1, 1, (3, 4, 5))
+    halo_start(E, 1, 1, UP)
     conv2(SIDES)
-    halo_start(E, 1, 1, (6, 7))
+    halo_start(E, 1, 1, ACROSS)
     conv2(INNER)
 
     def shifted(e):
@@ -301,18 +338,16 @@
             out[t] = jnp.concatenate([flat[at] for flat in shares], 0).astype(bf16)
 
     def scatter(k, src):
-        def send(n, carry):
-            to = (tile + n) % 16
-            owner = (2 * (to // GZ) + k) * GZ + to % GZ
+        def send(a, b):
+            to = (half if a == 0 else 1 - half) * GZ + zs_at[b]
             pltpu.make_async_remote_copy(
                 src_ref=src.at[to],
-                dst_ref=R.at[(place - owner + PLANE) % PLANE],
+                dst_ref=R.at[16 * a + 2 * b + jnp.where(core == k, 0, 1)],
                 send_sem=gs.at[k],
                 recv_sem=gr,
-                device_id=plane_device(owner),
+                device_id=(2 * (half if a == 0 else 1 - half) + k, zs_at[b], fs),
                 device_id_type=MESH,
             ).start()
-            return carry
 
         @pl.when(core == k)
         def _():
@@ -322,7 +357,10 @@
         def _():
             send(0, 0)
 
-        lax.fori_loop(1, 16, send, 0)
+        for b in range(GZ):
+            for a in range(2):
+                if a or b:
+                    send(a, b)
 
         def sent():
             for count, mine in ((15, core == k), (16, core != k)):
@@ -330,7 +368,7 @@
                 def _():
                     pltpu.make_async_remote_copy(
                         src_ref=src.at[pl.ds(0, count)], dst_ref=R.at[pl.ds(0, count)],
-                        send_sem=gs.at[k], recv_sem=gr, device_id=plane_device(place),
+                        send_sem=gs.at[k], recv_sem=gr, device_id=(gy, gz, fs),
                         device_id_type=MESH,
                     ).wait_send()
 
@@ -339,7 +377,7 @@
             def _():
                 pltpu.make_async_remote_copy(
                     src_ref=R.at[pl.ds(1, PLANE - 1)], dst_ref=R.at[pl.ds(1, PLANE - 1)],
-                    send_sem=gs.at[k], recv_sem=gr, device_id=plane_device(place),
+                    send_sem=gs.at[k], recv_sem=gr, device_id=(gy, gz, fs),
                     device_id_type=MESH,
                 ).wait_recv()
 
@@ -369,7 +407,7 @@
 
     back(INNER)
     G[...] = weight_grad(X, 2, own_error, [sum(INNER, ())])
-    settle(("halo", 1))
+    halo_settle(1, DOWN + UP + ACROSS)
     rim = LOW + HIGH + SIDES
     back(rim)
     grad1 = G[...] + weight_grad(X, 2, own_error, [sum(rim[:5], ()), sum(rim[5:], ())])
@@ -389,12 +427,12 @@
     def along(n, owner):
         return pltpu.make_async_remote_copy(
             src_ref=Z.at[owner], dst_ref=Z.at[owner], send_sem=zs.at[n - 1],
-            recv_sem=zr.at[n - 1], device_id=(gy, gz, (fs + n) % NF), device_id_type=MESH,
+            recv_sem=zr.at[n - 1], device_id=(gy, gz, fs_at[n]), device_id_type=MESH,
         )
 
     def sums():
         for n in range(1, NF):
-            along(n, (fs - n + NF) % NF).wait_recv()
+            along(n, fs_at[NF - n]).wait_recv()
 
     def sums_sent():
         for n in range(1, NF):
@@ -415,19 +453,19 @@
     slot = core * 16 + tile
     A[slot] = Q[...]
 
-    def spread(n, carry):
+    for a, b in others:
         pltpu.make_async_remote_copy(
             src_ref=Q, dst_ref=A.at[slot], send_sem=qs, recv_sem=qr,
-            device_id=plane_device((place + n) % PLANE), device_id_type=MESH,
+            device_id=(ys[a], zs_at[b], fs), device_id_type=MESH,
         ).start()
-        return carry
-
-    lax.fori_loop(1, PLANE, spread, 0)
     gather = pltpu.make_async_remote_copy(
         src_ref=A.at[pl.ds(0, PLANE - 1)], dst_ref=A.at[pl.ds(0, PLANE - 1)],
-        send_sem=qs, recv_sem=qr, device_id=plane_device(place), device_id_type=MESH,
+        send_sem=qs, recv_sem=qr, device_id=(gy, gz, fs), device_id_type=MESH,
     )
     owed["gather"], owed["gather sent"] = gather.wait_recv, gather.wait_send
+    for name in list(owed):
+        if name not in ("gather", "gather sent"):
+            settle(name)
     settle("gather")
 
     tiles = [A[n].astype(f32) for n in range(PLANE)]
@@ -436,8 +474,6 @@
         squares = squares + tile_in[8:]
     norm = jnp.sqrt(jnp.sum(squares, keepdims=True))
     factor = jnp.minimum(1.0, 1.0 / (norm + 1e-06))
-    for n in range(4, 8):
-        settle(("load", n))
     for k, (m_ref, s_ref, u_ref) in enumerate(
         ((m1_ref, s1_ref, u1_ref), (m2_ref, s2_ref, u2_ref))
     ):

time: 42.9 us -> 42.3 us (0.986)
  Pallas kernels: 42.1 us -> 41.6 us
    pallas_call x1, Pallas kernels: 41.3 us -> 40.7 us  [shards(): pl.pallas_call(kernel, out_shape=[pltpu.VMEM(r.shape, r.dtype) for r in r...]
where the time goes in v5:
time: 42.3 us; the launch traced here: 42.2 us
  Pallas kernels  41.6 us (98%)
  between operations  0.64 us (2%)
    pallas_call x1, Pallas kernels, shards(): pl.pallas_call(kernel, out_shape=[pltpu.VMEM(r.shape, r.dtype) for r in r...  40.7 us

profile of v5, /device:TPU:1, one launch (start us, length us, event | category | flops | bytes accessed | tf_op | source)
XLA Modules:
  0.0 42.2 jit_solution(10434742911640502128)
XLA Ops:
  0.6 40.7 %shard_map.103 = (bf16[48,4,8,128]{3,2,1,0:T(8,128)(2,1)S(1)}, f32[48,324]{1,0:T(8,128)S(1)}, f32[48,324]{1,0:T(8,128)S(1)}) custom-call(bf16[48,4,8,128]{3,2,1,0:T(8,128)(2,1)} %bitcast.3, bf16[48,4,8,128]{3,2,1,0:T(8,128)(2,1)} %bitcast.4, f32[48,324]{1,0:T(8,128)} %k1_hbm.1, f32[48,324]{1,0:T(8,128)} %k2_hbm.1, f32[48,324]{1,0:T(8,128)} %m1_hbm.1, ...), custom_call_target="tpu_custom_call" | custom-call | tf_op jit(solution)/shard_map/pallas_call | solution.py:520
  41.4 0.8 %shard_map.104 = (bf16[48,4,8,128]{3,2,1,0:T(8,128)(2,1)}, f32[48,324]{1,0:T(8,128)}, f32[48,324]{1,0:T(8,128)}) custom-call(bf16[48,4,8,128]{3,2,1,0:T(8,128)(2,1)S(1)} %get-tuple-element.9.refs_0_, f32[48,324]{1,0:T(8,128)S(1)} %get-tuple-element.10.refs_1_, f32[48,324]{1,0:T(8,128)S(1)} %get-tuple-element.11.refs_2_), custom_call_target="tpu_custom_call" | custom-call | tf_op jit(solution)/shard_map/pallas_call | solution.py:560

commit v6 on v5

--- a/solution.py
+++ b/solution.py
@@ -109,13 +109,13 @@
     ys, zs_at, fs_at = further(gy, GY), further(gz, GZ), further(fs, NF)
     others = [(a, b) for b in range(GZ) for a in range(GY)][1:]
 
+    for n in range(1, NF):
+        pl.semaphore_signal(
+            barrier, inc=1, device_id=(gy, gz, fs_at[n]), device_id_type=MESH
+        )
     for a, b in others:
         pl.semaphore_signal(
             barrier, inc=1, device_id=(ys[a], zs_at[b], fs), device_id_type=MESH
-        )
-    for n in range(1, NF):
-        pl.semaphore_signal(
-            barrier, inc=1, device_id=(gy, gz, fs_at[n]), device_id_type=MESH
         )
 
     for k, ref in enumerate((k1_ref, k2_ref)):
@@ -410,7 +410,7 @@
     halo_settle(1, DOWN + UP + ACROSS)
     rim = LOW + HIGH + SIDES
     back(rim)
-    grad1 = G[...] + weight_grad(X, 2, own_error, [sum(rim[:5], ()), sum(rim[5:], ())])
+    grad1 = G[...] + weight_grad(X, 2, own_error, [sum(rim, ())])
     pack(grad1, P1)
     scatter(0, P1)
 
@@ -422,7 +422,7 @@
     own = R[0].astype(f32)
     for n in range(1, PLANE):
         own = own + R[n].astype(f32)
-    Z[fs] = own.reshape(NF, 8, 128)
+    Z[fs] = own.astype(bf16)
 
     def along(n, owner):
         return pltpu.make_async_remote_copy(
@@ -442,7 +442,7 @@
         along(n, fs).start()
     owed["sums"], owed["sums sent"] = sums, sums_sent
     settle("sums")
-    total = Z[0] + Z[1] + Z[2] + Z[3]
+    total = sum(Z[n].astype(f32) for n in range(NF)).reshape(NF, 8, 128)
     TT[...] = total
     squares = jnp.sum(jnp.sum(total * total, 0), 0, keepdims=True)
     rounded = squares.astype(bf16).astype(f32)
@@ -540,7 +540,7 @@
             pltpu.VMEM((16, NF * 8, 128), bf16),
             pltpu.VMEM((16, NF * 8, 128), bf16),
             pltpu.VMEM((PLANE, NF * 8, 128), bf16),
-            pltpu.VMEM((NF, NF, 8, 128), f32),
+            pltpu.VMEM((NF, NF * 8, 128), bf16),
             pltpu.VMEM((NF, 8, 128), f32),
             pltpu.VMEM((16, 128), bf16),
             pltpu.VMEM((PLANE, 16, 128), bf16),

time: 42.3 us -> 42.2 us (level)
  no operation moved by 1% of the time
where the time goes in v6:
time: 42.2 us; the launch traced here: 42 us
  Pallas kernels  41.4 us (98%)
  between operations  0.64 us (2%)
    pallas_call x1, Pallas kernels, shards(): pl.pallas_call(kernel, out_shape=[pltpu.VMEM(r.shape, r.dtype) for r in r...  40.6 us

profile of v6, /device:TPU:1, one launch (start us, length us, event | category | flops | bytes accessed | tf_op | source)
XLA Modules:
  0.0 42.0 jit_solution(3160412054668189127)
XLA Ops:
  0.6 40.6 %shard_map.103 = (bf16[48,4,8,128]{3,2,1,0:T(8,128)(2,1)S(1)}, f32[48,324]{1,0:T(8,128)S(1)}, f32[48,324]{1,0:T(8,128)S(1)}) custom-call(bf16[48,4,8,128]{3,2,1,0:T(8,128)(2,1)} %bitcast.3, bf16[48,4,8,128]{3,2,1,0:T(8,128)(2,1)} %bitcast.4, f32[48,324]{1,0:T(8,128)} %k1_hbm.1, f32[48,324]{1,0:T(8,128)} %k2_hbm.1, f32[48,324]{1,0:T(8,128)} %m1_hbm.1, ...), custom_call_target="tpu_custom_call" | custom-call | tf_op jit(solution)/shard_map/pallas_call | solution.py:520
  41.2 0.8 %shard_map.104 = (bf16[48,4,8,128]{3,2,1,0:T(8,128)(2,1)}, f32[48,324]{1,0:T(8,128)}, f32[48,324]{1,0:T(8,128)}) custom-call(bf16[48,4,8,128]{3,2,1,0:T(8,128)(2,1)S(1)} %get-tuple-element.9.refs_0_, f32[48,324]{1,0:T(8,128)S(1)} %get-tuple-element.10.refs_1_, f32[48,324]{1,0:T(8,128)S(1)} %get-tuple-element.11.refs_2_), custom_call_target="tpu_custom_call" | custom-call | tf_op jit(solution)/shard_map/pallas_call | solution.py:560

commit v7 on v6

--- a/solution.py
+++ b/solution.py
@@ -274,13 +274,13 @@
     conv1(INNER)
     halo_settle(0, ACROSS)
     relay_start(X, 2, 0)
-    settle(("weight", 1))
-    full2 = gathered(1)
-    forward_matrix(full2, W2)
     conv1(WIDE_Z)
     halo_settle(0, DOWN + UP)
     conv1(WIDE)
     clear_outside(H, 1)
+    settle(("weight", 1))
+    full2 = gathered(1)
+    forward_matrix(full2, W2)
 
     def conv2(groups):
         for cells in groups:

time: 42.2 us -> 42.3 us (level)
  no operation moved by 1% of the time
where the time goes in v7:
time: 42.3 us; the launch traced here: 42.2 us
  Pallas kernels  41.5 us (98%)
  between operations  0.64 us (2%)
    pallas_call x1, Pallas kernels, shards(): pl.pallas_call(kernel, out_shape=[pltpu.VMEM(r.shape, r.dtype) for r in r...  40.7 us

profile of v7, /device:TPU:1, one launch (start us, length us, event | category | flops | bytes accessed | tf_op | source)
XLA Modules:
  0.0 42.2 jit_solution(719490007718606221)
XLA Ops:
  0.6 40.7 %shard_map.103 = (bf16[48,4,8,128]{3,2,1,0:T(8,128)(2,1)S(1)}, f32[48,324]{1,0:T(8,128)S(1)}, f32[48,324]{1,0:T(8,128)S(1)}) custom-call(bf16[48,4,8,128]{3,2,1,0:T(8,128)(2,1)} %bitcast.3, bf16[48,4,8,128]{3,2,1,0:T(8,128)(2,1)} %bitcast.4, f32[48,324]{1,0:T(8,128)} %k1_hbm.1, f32[48,324]{1,0:T(8,128)} %k2_hbm.1, f32[48,324]{1,0:T(8,128)} %m1_hbm.1, ...), custom_call_target="tpu_custom_call" | custom-call | tf_op jit(solution)/shard_map/pallas_call | solution.py:520
  41.3 0.8 %shard_map.104 = (bf16[48,4,8,128]{3,2,1,0:T(8,128)(2,1)}, f32[48,324]{1,0:T(8,128)}, f32[48,324]{1,0:T(8,128)}) custom-call(bf16[48,4,8,128]{3,2,1,0:T(8,128)(2,1)S(1)} %get-tuple-element.9.refs_0_, f32[48,324]{1,0:T(8,128)S(1)} %get-tuple-element.10.refs_1_, f32[48,324]{1,0:T(8,128)S(1)} %get-tuple-element.11.refs_2_), custom_call_target="tpu_custom_call" | custom-call | tf_op jit(solution)/shard_map/pallas_call | solution.py:560
